TPU v7x, 32 devices: a whole 2x2x4 slice. The times are simulated.
32 devices in a mesh: seq: 8 (over z, x), dp: 4 (over y, core).
Axes of the slice: x: 2, y: 2, z: 4, core: 2. Of those that a mesh axis runs over, the one named last changes fastest.
Arguments:
- tokens: bfloat16 [4, 8192, 512], P('dp', 'seq'), may hold values from -6 to 6
- lengths: int32 [4, 3], P('dp'), may hold values from 256 to 7424, as said below
- gain: float32 [512], replicated, may hold values from 0.5 to 1.5
- b_proj: bfloat16 [2, 512, 256], replicated, may hold values from -0.25 to 0.25
- c_proj: bfloat16 [2, 256, 512], replicated, may hold values from -0.25 to 0.25
- skip: float32 [512], replicated, may hold values from -3 to 3
- nu: float32 [256], replicated, may hold values from -12 to -3
- theta: float32 [256], replicated, may hold values from -2.5 to 0
- gamma_log: float32 [256], replicated, may hold values from -7 to 0
- glu: bfloat16 [512, 1024], replicated, may hold values from -0.25 to 0.25
- out_grad: bfloat16 [4, 8192, 512], P('dp', 'seq'), may hold values from -6 to 6
Outputs:
- block_out: bfloat16 [4, 8192, 512], P('dp', 'seq')
- in_grad: bfloat16 [4, 8192, 512], P('dp', 'seq')
- gain_grad: float32 [512], replicated
- b_grad: float32 [2, 512, 256], replicated
- c_grad: float32 [2, 256, 512], replicated
- skip_grad: float32 [512], replicated
- nu_grad: float32 [256], replicated
- theta_grad: float32 [256], replicated
- gamma_grad: float32 [256], replicated
- glu_grad: float32 [512, 1024], replicated
Inputs may be any that keep to these rules, and one draw needn't show every extreme that they name: Each row holds 3 lengths summing to 8192: 256, 512 and 7424, in an order drawn from the seed.
All inputs are finite; a program needn't handle non-finite values.
Results may differ from a plain program's by a relative error of at most 0.02.
Values may be sent and summed in bfloat16 or wider, within the bound.
A program may use at most 128 MiB of HBM per device.

v0:
```python
import functools
import math

import jax
import jax.numpy as jnp
from jax import lax
from jax.experimental import pallas as pl
from jax.experimental.pallas import tpu as pltpu
from jax.sharding import PartitionSpec as P

MESH = pl.DeviceIdType.MESH
F32, BF16 = jnp.float32, jnp.bfloat16
EPS = 1e-5
RESET = 256
TILE = 256
BLOCKS = 16
LANES = 128
ROWS = 512
NT = (((1,), (1,)), ((), ()))
TN = (((0,), (0,)), ((), ()))


def mm(a, b, dims=(((1,), (0,)), ((), ()))):
    return lax.dot_general(a, b, dims, preferred_element_type=F32)


def cmul(a, b):
    return a[0] * b[0] - a[1] * b[1], a[0] * b[1] + a[1] * b[0]


def cpow2(a, times):
    for _ in range(times):
        a = cmul(a, a)
    return a


def fold(value):
    return jnp.sum(value.reshape(-1, 8, value.shape[1]), axis=0)


class Place:
    def __init__(self, seq, dp):
        self.seq, self.dp = seq, dp
        self.nx = max(1, math.isqrt(seq // 2))
        self.nz = seq // self.nx
        self.ny = dp // 2
        self.np = self.nx * self.ny
        self.s, self.d = lax.axis_index("seq"), lax.axis_index("dp")
        self.z, self.x = self.s // self.nx, lax.rem(self.s, self.nx)
        self.y, self.c = self.d // 2, lax.rem(self.d, 2)
        self.p = self.x * self.ny + self.y

    def core(self):
        return (self.s, self.y * 2 + 1 - self.c)

    def plane(self, p):
        return (self.z * self.nx + p // self.ny, lax.rem(p, self.ny) * 2 + self.c)

    def line(self, z):
        return (z * self.nx + self.x, self.d)

    def group(self, s):
        return (s, self.d)


def remote(src, dst, send, recv, device):
    return pltpu.make_async_remote_copy(
        src_ref=src, dst_ref=dst, send_sem=send, recv_sem=recv, device_id=device, device_id_type=MESH
    )


class Sum:
    def __init__(self, at, part, out, rc, sc, rx, sx, rz, send, recv):
        self.at, self.part, self.out = at, part, out
        self.rc, self.sc, self.rx, self.sx, self.rz = rc, sc, rx, sx, rz
        self.send, self.recv = send, recv
        self.sent, self.slot, self.pending = [], 0, []
        self.half = ROWS // 2
        self.quarter = self.half // at.np
        self.piece = self.quarter // at.nz
        self.scatter = self.piece % 16 == 0
        self.row0 = pl.multiple_of(at.c * self.half, 16)
        self.row1 = pl.multiple_of(self.row0 + at.p * self.quarter, 16)
        if self.scatter:
            self.row2 = pl.multiple_of(self.row1 + at.z * self.piece, 16)

    def go(self, src, dst, device):
        copy = remote(src, dst, self.send.at[self.slot], self.recv.at[self.slot], device)
        self.slot += 1
        copy.start()
        self.sent.append(copy)
        self.pending.append(copy)

    def arrive(self):
        for copy in self.pending:
            copy.wait_recv()
        self.pending = []

    def start_core(self):
        other = pl.multiple_of((1 - self.at.c) * self.half, 16)
        self.go(self.part.at[pl.ds(other, self.half)], self.rc, self.at.core())

    def start_plane(self):
        at = self.at
        self.arrive()
        own = self.part[pl.ds(self.row0, self.half), :].astype(F32)
        self.sc[...] = (own + self.rc[...].astype(F32)).astype(BF16)
        for o in range(1, at.np):
            p = lax.rem(at.p + o, at.np)
            rows = pl.ds(pl.multiple_of(p * self.quarter, 16), self.quarter)
            self.go(self.sc.at[rows], self.rx.at[o - 1], at.plane(p))

    def start_line(self):
        at = self.at
        self.arrive()
        total = self.sc[pl.ds(pl.multiple_of(at.p * self.quarter, 16), self.quarter), :].astype(F32)
        for o in range(1, at.np):
            total += self.rx[o - 1].astype(F32)
        if self.scatter:
            self.sx[...] = total.astype(BF16)
            for o in range(1, at.nz):
                z = lax.rem(at.z + o, at.nz)
                rows = pl.ds(pl.multiple_of(z * self.piece, 16), self.piece)
                self.go(self.sx.at[rows], self.rz.at[o - 1], at.line(z))
        else:
            self.rz[at.z] = total.astype(BF16)
            for o in range(1, at.nz):
                self.go(self.rz.at[at.z], self.rz.at[at.z], at.line(lax.rem(at.z + o, at.nz)))

    def back_line(self):
        at = self.at
        self.arrive()
        if not self.scatter:
            return
        total = self.sx[pl.ds(pl.multiple_of(at.z * self.piece, 16), self.piece), :].astype(F32)
        for o in range(1, at.nz):
            total += self.rz[o - 1].astype(F32)
        mine = pl.ds(self.row2, self.piece)
        self.out[mine, :] = total.astype(BF16)
        for o in range(1, at.nz):
            self.go(self.out.at[mine], self.out.at[mine], at.line(lax.rem(at.z + o, at.nz)))

    def back_plane(self):
        at = self.at
        mine = pl.ds(self.row1, self.quarter)
        if self.scatter:
            self.arrive()
        else:
            total = self.rz[0].astype(F32)
            for z in range(1, at.nz):
                total += self.rz[z].astype(F32)
            self.out[mine, :] = total.astype(BF16)
        for o in range(1, at.np):
            self.go(self.out.at[mine], self.out.at[mine], at.plane(lax.rem(at.p + o, at.np)))

    def back_core(self):
        self.arrive()
        mine = pl.ds(self.row0, self.half)
        self.go(self.out.at[mine], self.out.at[mine], self.at.core())

    def drain(self):
        for copy in self.sent:
            copy.wait_send()


def kernel(
    seq, dp,
    tok_hbm, og_hbm, b_hbm, c_hbm, glu_hbm, len_ref, gain_ref, skip_ref, nu_ref, theta_ref, gam_ref,
    block_hbm, ing_hbm, grads_ref, small_ref,
    tok, og, bw, cw, gw, bout, xhat, rstd, u, x, h, hl, g, dz, dy, dh,
    edge, init, msg, rmsg, part, rc, sc, rx, sx, rz, sm, smz,
    load_sem, store_sem, msend, mrecv, asend, arecv, ssend, srecv,
):
    at = Place(seq, dp)
    tokens, width = tok.shape
    chan = width // 2
    step = tokens // BLOCKS
    tiles = tokens // TILE
    lo, hi = slice(0, chan), slice(chan, width)

    loads = []

    def load(src, dst):
        copy = pltpu.make_async_copy(src, dst, load_sem.at[len(loads)])
        copy.start()
        loads.append(copy)
        return copy

    tok_in = [load(tok_hbm.at[0, pl.ds(i * TILE, TILE)], tok.at[pl.ds(i * TILE, TILE)]) for i in range(tiles)]
    b_in = [load(b_hbm.at[k], bw.at[:, pl.ds(k * chan, chan)]) for k in range(2)]
    c_in = [load(c_hbm.at[k], cw.at[pl.ds(k * chan, chan)]) for k in range(2)]
    glu_in = load(glu_hbm, gw)
    og_in = load(og_hbm.at[0], og)

    barrier = pltpu.get_barrier_semaphore()
    peers = [at.core()] + [at.group(lax.rem(at.s + o, seq)) for o in range(1, seq)]
    for oy in range(1, at.ny):
        for ox in range(at.nx):
            y, xx = lax.rem(at.y + oy, at.ny), lax.rem(at.x + ox, at.nx)
            peers.append((at.z * at.nx + xx, y * 2 + at.c))
    for peer in peers:
        pl.semaphore_signal(barrier, inc=1, device_id=peer, device_id_type=MESH)

    modulus = jnp.exp(-jnp.exp(nu_ref[...]))
    angle = jnp.exp(theta_ref[...])
    lam = (modulus * jnp.cos(angle), modulus * jnp.sin(angle))
    conj = (lam[0], -lam[1])
    lam_step = cpow2(lam, int(math.log2(step)))
    lam_all = cpow2(lam_step, int(math.log2(BLOCKS)))
    conj_step, conj_all = (lam_step[0], -lam_step[1]), (lam_all[0], -lam_all[1])
    scaling = jnp.exp(gam_ref[...])
    scale2 = jnp.concatenate([scaling, -scaling], axis=1)

    starts, total = [], jnp.int32(0)
    for k in range(len_ref.shape[1]):
        starts.append(total)
        total = total + len_ref[0, k]

    def keep_at(position):
        hit = functools.reduce(jnp.logical_or, [position == start for start in starts])
        return jnp.where(hit, 0.0, 1.0).astype(F32)

    def keep_all(device):
        first = device * tokens
        hits = [jnp.logical_and(start >= first, start < first + tokens) for start in starts]
        return jnp.where(functools.reduce(jnp.logical_or, hits), 0.0, 1.0).astype(F32)

    block_keep = [
        keep_at(at.s * tokens + k * step) if (k * step) % RESET == 0 else None for k in range(BLOCKS)
    ]

    def kept(k, value):
        if block_keep[k] is None:
            return value
        return value[0] * block_keep[k], value[1] * block_keep[k]

    def put(ref, rows, value):
        for k in range(width // LANES):
            ref[k, rows, :] = value[:, k * LANES : (k + 1) * LANES]

    def take(ref, rows):
        return jnp.concatenate([ref[k, rows, :] for k in range(width // LANES)], axis=1)

    gain = gain_ref[...]
    skip = skip_ref[...]
    for copy in b_in:
        copy.wait()
    for i in range(tiles):
        tok_in[i].wait()

    def front(i, carry):
        rows = pl.ds(pl.multiple_of(i * TILE, TILE), TILE)
        value = tok[rows, :].astype(F32)
        centered = value - jnp.mean(value, axis=1, keepdims=True)
        inv = lax.rsqrt(jnp.mean(centered * centered, axis=1, keepdims=True) + EPS)
        normal = centered * inv
        xhat[rows, :] = normal
        rstd[rows, :] = inv
        low = (normal * gain).astype(BF16)
        u[rows, :] = low
        put(x, rows, mm(low, bw[...]).astype(BF16).astype(F32) * scale2)
        return carry

    lax.fori_loop(0, tiles, front, 0)

    def add(a, b):
        return a[0] + b[0], a[1] + b[1]

    halves = chan // LANES

    def rows_of(j):
        return pl.ds(j, BLOCKS, stride=step)

    zeros = jnp.zeros((BLOCKS, chan), F32)

    def strided(ref, j):
        return take_half(ref, rows_of(j), 0), take_half(ref, rows_of(j), halves)

    def take_half(ref, rows, first):
        return jnp.concatenate([ref[first + k, rows, :] for k in range(halves)], axis=1)

    def put_strided(ref, j, value):
        for k in range(halves):
            ref[k, rows_of(j), :] = value[0][:, k * LANES : (k + 1) * LANES]
            ref[halves + k, rows_of(j), :] = value[1][:, k * LANES : (k + 1) * LANES]

    def advance(j, carry):
        return add(cmul(conj, carry), strided(x, j))

    last = lax.fori_loop(0, step, advance, (zeros, zeros), unroll=8)
    edge[:, lo], edge[:, hi] = last

    zero_row = (jnp.zeros((1, chan), F32), jnp.zeros((1, chan), F32))

    def edge_row(k):
        return edge[k : k + 1, lo], edge[k : k + 1, hi]

    state = zero_row
    for k in range(BLOCKS):
        state = add(edge_row(k), cmul(conj_step, kept(k, state)))

    def exchange(which, value):
        msg[which, :, lo], msg[which, :, hi] = value
        copies = []
        for o in range(seq - 1, 0, -1):
            copy = remote(
                msg.at[which], rmsg.at[which, o], msend.at[which, o], mrecv.at[which, o],
                at.group(lax.rem(at.s + o, seq)),
            )
            copy.start()
            copies.append(copy)
        return copies

    def gather(which, factor, copies, ahead):
        for copy in copies:
            copy.wait_recv()
        result = zero_row
        for o in range(seq - 1, 0, -1):
            source = at.s + o if ahead else at.s - o
            slot = seq - o if ahead else o
            there = (rmsg[which, slot, :, lo], rmsg[which, slot, :, hi])
            k = keep_all(source)
            new = add(there, cmul((factor[0] * k, factor[1] * k), result))
            valid = source < seq if ahead else source >= 0
            result = tuple(jnp.where(valid, a, b) for a, b in zip(new, result))
        return result

    pl.semaphore_wait(barrier, len(peers))
    sent_forward = exchange(0, state)
    carry = gather(0, conj_all, sent_forward, False)

    for k in range(BLOCKS):
        begin = kept(k, carry)
        init[k : k + 1, lo], init[k : k + 1, hi] = begin
        if k + 1 < BLOCKS:
            carry = add(edge_row(k), cmul(conj_step, begin))

    def advance_store(j, carry):
        carry = advance(j, carry)
        put_strided(h, j, carry)
        return carry

    lax.fori_loop(0, step, advance_store, (init[:, lo], init[:, hi]), unroll=8)

    for copy in c_in:
        copy.wait()
    glu_in.wait()
    og_in.wait()

    def middle(i, skip_sum):
        rows = pl.ds(pl.multiple_of(i * TILE, TILE), TILE)
        low = take(h, rows).astype(BF16)
        hl[rows, :] = low
        ul = u[rows, :].astype(F32)
        v = mm(low, cw[...]) + skip * ul
        square = v * v
        t = jnp.tanh(0.7978845608028654 * (v + 0.044715 * v * square))
        half = 0.5 * (1.0 + t)
        gl = (v * half).astype(BF16)
        slope = half + 0.5 * v * (1.0 - t * t) * (0.7978845608028654 * (1.0 + 3 * 0.044715 * square))
        g[rows, :] = gl
        value = mm(gl, gw[:, :width])
        s = jax.nn.sigmoid(mm(gl, gw[:, width:]))
        branch = value * s
        bout[rows, :] = (tok[rows, :].astype(F32) + branch).astype(BF16)
        cot = og[rows, :].astype(F32)
        dvalue = (cot * s).astype(BF16)
        dgate = (cot * branch * (1.0 - s)).astype(BF16)
        dz[rows, :width] = dvalue
        dz[rows, width:] = dgate
        back = mm(dvalue, gw[:, :width], NT) + mm(dgate, gw[:, width:], NT)
        dyl = (back * slope).astype(BF16)
        dy[rows, :] = dyl
        put(dh, rows, mm(dyl, cw[...], NT).astype(BF16).astype(F32))
        return skip_sum + fold(dyl.astype(F32) * ul)

    skip_sum = lax.fori_loop(0, tiles, middle, jnp.zeros((8, width), F32))
    out_block = pltpu.make_async_copy(bout, block_hbm.at[0], store_sem.at[0])
    out_block.start()

    def retreat(k, carry):
        j = step - 1 - k
        return cmul(lam, add(strided(dh, j), carry))

    first = lax.fori_loop(0, step, retreat, (zeros, zeros), unroll=8)
    edge[:, lo], edge[:, hi] = first
    state = zero_row
    for k in range(BLOCKS - 1, -1, -1):
        state = kept(k, add(edge_row(k), cmul(lam_step, state)))
    sent_backward = exchange(1, state)

    def stream(k):
        return Sum(
            at, part.at[k], grads_ref.at[k], rc.at[k], sc.at[k], rx.at[k], sx.at[k], rz.at[k],
            asend.at[k], arecv.at[k],
        )

    sums = [stream(k) for k in range(4)]
    part[0] = mm(g[...], dz[:, :width], TN).astype(BF16)
    sums[0].start_core()
    part[1] = mm(g[...], dz[:, width:], TN).astype(BF16)
    sums[1].start_core()
    part[2] = mm(hl[...], dy[...], TN).astype(BF16)
    sums[2].start_core()

    incoming = gather(1, lam_all, sent_backward, True)
    for k in range(BLOCKS - 1, -1, -1):
        edge_k = edge_row(k)
        if k > 0:
            following = kept(k, add(edge_k, cmul(lam_step, incoming)))
        edge[k : k + 1, lo], edge[k : k + 1, hi] = incoming
        if k > 0:
            incoming = following

    def adjoint(j, carry, before):
        sre, sim, pre, pim, gsum = carry
        wre, wim = add(strided(dh, j), (sre, sim))
        yre, yim = before
        xre, xim = strided(x, j)
        pre = pre + (yre * wre + yim * wim)
        pim = pim + (yim * wre - yre * wim)
        gsum = gsum + (xre * wre + xim * wim)
        put_strided(dh, j, (scaling * wre, -scaling * wim))
        sre, sim = cmul(lam, (wre, wim))
        return sre, sim, pre, pim, gsum

    def adjoint_step(k, carry):
        j = step - 1 - k
        return adjoint(j, carry, strided(h, j - 1))

    carry = lax.fori_loop(0, step - 1, adjoint_step, (edge[:, lo], edge[:, hi], zeros, zeros, zeros), unroll=7)
    carry = adjoint(0, carry, (init[:, lo], init[:, hi]))
    pre, pim, gsum = (jnp.sum(part_sum, axis=0, keepdims=True) for part_sum in carry[2:])

    def lower(i, carry):
        rows = pl.ds(pl.multiple_of(i * TILE, TILE), TILE)
        hl[rows, :] = take(dh, rows).astype(BF16)
        return carry

    lax.fori_loop(0, tiles, lower, 0)
    part[3] = mm(u[...], hl[...], TN).astype(BF16)
    sums[3].start_core()
    for one in sums:
        one.start_plane()

    def last_tile(i, gain_sum):
        rows = pl.ds(pl.multiple_of(i * TILE, TILE), TILE)
        du = mm(hl[rows, :], bw[...], NT) + skip * dy[rows, :].astype(F32)
        normal = xhat[rows, :]
        e = gain * du
        mean_e = jnp.mean(e, axis=1, keepdims=True)
        mean_ex = jnp.mean(e * normal, axis=1, keepdims=True)
        grad = og[rows, :].astype(F32) + (e - mean_e - normal * mean_ex) * rstd[rows, :]
        tok[rows, :] = grad.astype(BF16)
        return gain_sum + fold(du * normal)

    gain_sum = lax.fori_loop(0, tiles, last_tile, jnp.zeros((8, width), F32))
    out_ing = pltpu.make_async_copy(tok, ing_hbm.at[0], store_sem.at[1])
    out_ing.start()

    small = [
        jnp.sum(gain_sum, axis=0, keepdims=True),
        jnp.sum(skip_sum, axis=0, keepdims=True),
        jnp.concatenate(
            [
                -jnp.exp(nu_ref[...]) * (lam[0] * pre + lam[1] * pim),
                angle * (lam[0] * pim - lam[1] * pre),
            ],
            axis=1,
        ),
        jnp.concatenate([gsum, gsum], axis=1),
        jnp.zeros((4, width), F32),
    ]
    small_slot = 0
    small_sent = []

    def spread(buffer, index, targets):
        nonlocal small_slot
        copies = []
        for target in targets:
            copy = remote(buffer.at[index], buffer.at[index], ssend.at[small_slot], srecv.at[small_slot], target)
            small_slot += 1
            copy.start()
            copies.append(copy)
        small_sent.extend(copies)
        return copies

    def collect(buffer, count, copies):
        for copy in copies:
            copy.wait_recv()
        value = buffer[0]
        for k in range(1, count):
            value = value + buffer[k]
        return value

    sm_core, sm_plane, sm_line = smz
    sm_core[at.c] = jnp.concatenate(small, axis=0)
    copies = spread(sm_core, at.c, [at.core()])
    for one in sums:
        one.start_line()
    sm_plane[at.p] = collect(sm_core, 2, copies)
    copies = spread(sm_plane, at.p, [at.plane(lax.rem(at.p + o, at.np)) for o in range(1, at.np)])
    for one in sums:
        one.back_line()
    sm_line[at.z] = collect(sm_plane, at.np, copies)
    copies = spread(sm_line, at.z, [at.line(lax.rem(at.z + o, at.nz)) for o in range(1, at.nz)])
    for one in sums:
        one.back_plane()
    small_ref[...] = collect(sm_line, at.nz, copies)
    for one in sums:
        one.back_core()
    for one in sums:
        one.arrive()
    for one in sums:
        one.drain()
    for copy in sent_forward + sent_backward + small_sent:
        copy.wait_send()
    out_block.wait()
    out_ing.wait()


def on_device(seq, dp, tokens, lengths, gain, b_proj, c_proj, skip, nu, theta, gamma_log, glu, out_grad):
    _, count, width = tokens.shape
    chan = nu.shape[0]
    at_nx = max(1, math.isqrt(seq // 2))
    at_nz, at_np = seq // at_nx, at_nx * (dp // 2)
    quarter = ROWS // 2 // at_np
    piece = quarter // at_nz
    rz_shape = (4, at_nz - 1, piece, ROWS) if piece % 16 == 0 else (4, at_nz, quarter, ROWS)
    slots = 2 + 2 * (at_np - 1) + 2 * (at_nz - 1)
    small_slots = 1 + (at_np - 1) + (at_nz - 1)
    anywhere = pl.BlockSpec(memory_space=pl.ANY)
    vmem = pl.BlockSpec(memory_space=pltpu.VMEM)
    smem = pl.BlockSpec(memory_space=pltpu.SMEM)
    dma = pltpu.SemaphoreType.DMA
    scan = pltpu.VMEM((width // LANES, count, LANES), F32)
    wide, low = pltpu.VMEM((count, width), F32), pltpu.VMEM((count, width), BF16)
    block_out, in_grad, grads, small = pl.pallas_call(
        functools.partial(kernel, seq, dp),
        out_shape=(
            jax.ShapeDtypeStruct(tokens.shape, BF16),
            jax.ShapeDtypeStruct(tokens.shape, BF16),
            jax.ShapeDtypeStruct((4, ROWS, ROWS), BF16),
            jax.ShapeDtypeStruct((8, width), F32),
        ),
        in_specs=[anywhere] * 5 + [smem] + [vmem] * 5,
        out_specs=(anywhere, anywhere, vmem, vmem),
        scratch_shapes=[
            low, low,
            pltpu.VMEM((width, 2 * chan), BF16),
            pltpu.VMEM((2 * chan, width), BF16),
            pltpu.VMEM((width, 2 * width), BF16),
            low,
            wide,
            pltpu.VMEM((count, 1), F32),
            low,
            scan, scan,
            low, low,
            pltpu.VMEM((count, 2 * width), BF16),
            low,
            scan,
            pltpu.VMEM((BLOCKS, 2 * chan), F32),
            pltpu.VMEM((BLOCKS, 2 * chan), F32),
            pltpu.VMEM((2, 1, 2 * chan), F32),
            pltpu.VMEM((2, seq, 1, 2 * chan), F32),
            pltpu.VMEM((4, ROWS, ROWS), BF16),
            pltpu.VMEM((4, ROWS // 2, ROWS), BF16),
            pltpu.VMEM((4, ROWS // 2, ROWS), BF16),
            pltpu.VMEM((4, at_np - 1, quarter, ROWS), BF16),
            pltpu.VMEM((4, quarter, ROWS), BF16),
            pltpu.VMEM(rz_shape, BF16),
            pltpu.VMEM((8, width), F32),
            (
                pltpu.VMEM((2, 8, width), F32),
                pltpu.VMEM((at_np, 8, width), F32),
                pltpu.VMEM((at_nz, 8, width), F32),
            ),
            dma((12,)),
            dma((2,)),
            dma((2, seq)),
            dma((2, seq)),
            dma((4, slots)),
            dma((4, slots)),
            dma((small_slots,)),
            dma((small_slots,)),
        ],
        compiler_params=pltpu.CompilerParams(
            collective_id=0, has_side_effects=True, vmem_limit_bytes=56 * 2**20
        ),
    )(
        tokens, out_grad, b_proj, c_proj, glu, lengths,
        gain[None], skip[None], nu[None], theta[None], gamma_log[None],
    )
    grads = grads.astype(F32)
    b_grad = jnp.stack([grads[3][:, :chan], grads[3][:, chan:]])
    c_grad = grads[2].reshape(2, chan, width)
    glu_grad = jnp.concatenate([grads[0], grads[1]], axis=1)
    return (
        block_out, in_grad, small[0], b_grad, c_grad, small[1],
        small[2, :chan], small[2, chan:], small[3, :chan], glu_grad,
    )


def solution(mesh):
    rows, whole = P("dp", "seq", None), P()
    return jax.shard_map(
        functools.partial(on_device, mesh.shape["seq"], mesh.shape["dp"]),
        mesh=mesh,
        in_specs=(rows, P("dp", None)) + (whole,) * 8 + (rows,),
        out_specs=(rows, rows) + (whole,) * 8,
        check_vma=False,
    )
```

profile of v0, /device:TPU:0, one launch (start us, length us, event | category | flops | bytes accessed | tf_op | source)
XLA Modules:
  0.0 80.3 jit_solution(13130617286656332102)
XLA Ops:
  0.6 68.8 %shard_map.186 = (bf16[1,1024,512]{2,1,0:T(8,128)(2,1)}, bf16[1,1024,512]{2,1,0:T(8,128)(2,1)}, bf16[4,512,512]{2,1,0:T(8,128)(2,1)}, f32[8,512]{1,0:T(8,128)}) custom-call(bf16[1,1024,512]{2,1,0:T(8,128)(2,1)} %tok_hbm.1, bf16[1,1024,512]{2,1,0:T(8,128)(2,1)} %og_hbm.1, bf16[2,512,256]{2,1,0:T(8,128)(2,1)} %b_hbm.1, bf16[2,256,512]{2,1,0:T(8,128)(2,1)} %c_hbm.1, ...), custom_call_target="tpu_custom_call" | custom-call | tf_op jit(solution)/shard_map/pallas_call | solution.py:538
  69.4 0.0 copy-start
  69.5 1.5 %fusion = (f32[1,256]{1,0:T(1,128)}, f32[1,256]{1,0:T(1,128)}, f32[1,256]{1,0:T(1,128)}) fusion(f32[8,512]{1,0:T(8,128)} %get-tuple-element.16), kind=kLoop, calls=%fused_computation.7 | loop fusion | bytes 6144 | tf_op jit(solution)/shard_map/slice | solution.py:600
  70.9 1.4 %fusion.1 = (f32[1,512]{1,0:T(1,128)}, f32[1,512]{1,0:T(1,128)}) fusion(f32[8,512]{1,0:T(8,128)} %get-tuple-element.16), kind=kLoop, calls=%fused_computation.8 | loop fusion | bytes 8192 | tf_op jit(solution)/shard_map/slice | solution.py:599
  72.3 2.1 %slice.48 = f32[1,512,512]{2,1,0:T(8,128)} slice(bf16[4,512,512]{2,1,0:T(8,128)(2,1)} %get-tuple-element.17), slice={[2:3], [0:512], [0:512]} | slice | bytes 2097152 | tf_op jit(solution)/shard_map/slice | solution.py:596
  74.4 0.0 copy-done
  74.4 0.6 convert_element_type.3
  75.0 0.3 slice_bitcast_fusion.1
  75.3 1.5 %pad_maximum_fusion = f32[512,1024]{1,0:T(8,128)} fusion(f32[512,512]{1,0:T(8,128)S(1)} %get-tuple-element.19, f32[512,512]{1,0:T(8,128)S(1)} %get-tuple-element.18), kind=kLoop, calls=%fused_computation | loop fusion | flops 524288 | bytes 4194304 | tf_op jit(solution)/shard_map/concatenate | solution.py:597
  76.8 0.0 copy-start.2
  76.8 0.1 slice_bitcast_fusion.4
  76.9 0.0 copy-start.1
  76.9 1.0 %pad_maximum_fusion.1 = f32[2,512,256]{2,1,0:T(8,128)} fusion(f32[1,512,256]{2,1,0:T(8,128)S(1)} %get-tuple-element.22, f32[1,512,256]{2,1,0:T(8,128)S(1)} %get-tuple-element.21), kind=kLoop, calls=%fused_computation.4 | loop fusion | flops 262144 | bytes 2097152 | tf_op jit(solution)/shard_map/stack | solution.py:595
  77.9 0.4 copy-done.2
  78.3 1.0 %copy.23 = bf16[1,1024,512]{2,1,0:T(8,128)(2,1)} copy(bf16[1,1024,512]{2,1,0:T(8,128)(2,1)S(1)} %copy-done.2) | data formatting | bytes 2097152
  79.3 0.0 copy-done.1
  79.3 1.0 %copy.24 = bf16[1,1024,512]{2,1,0:T(8,128)(2,1)} copy(bf16[1,1024,512]{2,1,0:T(8,128)(2,1)S(1)} %copy-done.1) | data formatting | bytes 2097152
Async XLA Ops:
  69.4 5.0 %copy-start = (bf16[4,512,512]{2,1,0:T(8,128)(2,1)S(1)}, bf16[4,512,512]{2,1,0:T(8,128)(2,1)}, u32[]{:S(2)}) copy-start(bf16[4,512,512]{2,1,0:T(8,128)(2,1)} %get-tuple-element.17) | copy-start | bytes 6291460
  76.8 1.6 %copy-start.2 = (bf16[1,1024,512]{2,1,0:T(8,128)(2,1)S(1)}, bf16[1,1024,512]{2,1,0:T(8,128)(2,1)}, u32[]{:S(2)}) copy-start(bf16[1,1024,512]{2,1,0:T(8,128)(2,1)} %get-tuple-element.38) | copy-start | bytes 3145732
  76.9 2.4 %copy-start.1 = (bf16[1,1024,512]{2,1,0:T(8,128)(2,1)S(1)}, bf16[1,1024,512]{2,1,0:T(8,128)(2,1)}, u32[]{:S(2)}) copy-start(bf16[1,1024,512]{2,1,0:T(8,128)(2,1)} %get-tuple-element.39) | copy-start | bytes 3145732
where the time goes:
time: 80.7 us; the launch traced here: 80.3 us
  Pallas kernels  68.8 us (85%)
  local copies, waits for them, and re-layouts  7.73 us (10%)
  other arithmetic  3.07 us (4%)
    pallas_call x1, Pallas kernels, on_device(): pl.pallas_call(functools.partial(kernel, seq, dp), out_shape=(jax.ShapeDt...  68.8 us
    unnamed x8, local copies, waits for them, and re-layouts  2.37 us
    slice x1, local copies, waits for them, and re-layouts, on_device(): c_grad = grads[2].reshape(2, chan, width)  2.14 us

commit v1 on v0

v1 whole, which is shorter than its diff:
```python
import functools
import math

import jax
import jax.numpy as jnp
from jax import lax
from jax.experimental import pallas as pl
from jax.experimental.pallas import tpu as pltpu
from jax.sharding import PartitionSpec as P

MESH = pl.DeviceIdType.MESH
F32, BF16 = jnp.float32, jnp.bfloat16
EPS = 1e-5
TILE = 256
LANES = 128
SUB = 8
STEPS = TILE // SUB
ROWS = 512
NT = (((1,), (1,)), ((), ()))
TN = (((0,), (0,)), ((), ()))


def mm(a, b, dims=(((1,), (0,)), ((), ()))):
    return lax.dot_general(a, b, dims, preferred_element_type=F32)


def add(a, b):
    return a[0] + b[0], a[1] + b[1]


def cmul(a, b):
    return a[0] * b[0] - a[1] * b[1], a[0] * b[1] + a[1] * b[0]


def cpow2(a, times):
    for _ in range(times):
        a = cmul(a, a)
    return a


def fold(value):
    return jnp.sum(value.reshape(-1, 8, value.shape[1]), axis=0)


class Place:
    def __init__(self, seq, dp):
        self.seq, self.dp = seq, dp
        self.nx = max(1, math.isqrt(seq // 2))
        self.nz = seq // self.nx
        self.ny = dp // 2
        plane = self.nx * self.ny
        self.zl = 2 if self.nz % 2 == 0 and (ROWS // 2 // (2 * plane)) % 16 == 0 else 1
        self.near_count, self.far_count = self.zl * plane, self.nz // self.zl

    def here(self):
        self.s, self.d = lax.axis_index("seq"), lax.axis_index("dp")
        self.z, self.x = self.s // self.nx, lax.rem(self.s, self.nx)
        self.y, self.c = self.d // 2, lax.rem(self.d, 2)
        self.zh, self.zo = self.z // self.zl, lax.rem(self.z, self.zl)
        self.q = (self.zo * self.nx + self.x) * self.ny + self.y
        return self

    def core(self):
        return (self.s, self.y * 2 + 1 - self.c)

    def near(self, o):
        q = lax.rem(self.q + o, self.near_count)
        z = self.zh * self.zl + q // (self.nx * self.ny)
        x = lax.rem(q // self.ny, self.nx)
        return (z * self.nx + x, lax.rem(q, self.ny) * 2 + self.c)

    def far(self, o):
        zh = lax.rem(self.zh + o, self.far_count)
        return ((zh * self.zl + self.zo) * self.nx + self.x, self.d)

    def group(self, o):
        return (lax.rem(self.s + o, self.seq), self.d)

    def peers(self):
        found = [self.core()] + [self.group(o) for o in range(1, self.seq)]
        for oy in range(1, self.ny):
            y = lax.rem(self.y + oy, self.ny)
            for zo in range(self.zl):
                for x in range(self.nx):
                    found.append(((self.zh * self.zl + zo) * self.nx + x, y * 2 + self.c))
        return found


def remote(src, dst, send, recv, device):
    return pltpu.make_async_remote_copy(
        src_ref=src, dst_ref=dst, send_sem=send, recv_sem=recv, device_id=device, device_id_type=MESH
    )


class Sum:
    def __init__(self, at, part, out, rc, sc, rx, fz, send, recv):
        self.at, self.part, self.out = at, part, out
        self.rc, self.sc, self.rx, self.fz = rc, sc, rx, fz
        self.send, self.recv = send, recv
        self.sent, self.slot = [], 0
        self.half = ROWS // 2
        self.piece = self.half // at.near_count
        self.row0 = pl.multiple_of(at.c * self.half, 16)

    def go(self, src, dst, device):
        copy = remote(src, dst, self.send.at[self.slot], self.recv.at[self.slot], device)
        self.slot += 1
        copy.start()
        self.sent.append(copy)
        return copy

    def place(self, q):
        return pl.multiple_of(lax.rem(q, self.at.near_count) * self.piece, 16)

    def rows(self, q):
        return pl.ds(pl.multiple_of(self.row0 + self.place(q), 16), self.piece)

    def start_core(self, left, right):
        for k in range(2):
            first = pl.multiple_of((1 - self.at.c if k == 0 else self.at.c) * self.half, self.half)
            rows = pl.ds(first, self.half)

            def columns(n, carry, rows=rows):
                cols = pl.ds(pl.multiple_of(n * self.half, self.half), self.half)
                self.part[rows, cols] = mm(left[:, rows], right[:, cols], TN).astype(BF16)
                return carry

            lax.fori_loop(0, ROWS // self.half, columns, 0)
            if k == 0:
                self.coming = [self.go(self.part.at[rows], self.rc, self.at.core())]

    def both(self, q):
        return self.part[self.rows(q), :].astype(F32) + self.rc[pl.ds(self.place(q), self.piece), :].astype(F32)

    def start_near(self):
        at = self.at
        self.coming[0].wait_recv()
        self.coming = []
        for o in range(1, at.near_count):
            self.sc[o - 1] = self.both(at.q + o).astype(BF16)
            self.coming.append(self.go(self.sc.at[o - 1], self.rx.at[o - 1], at.near(o)))

    def start_far(self):
        at = self.at
        total = self.both(at.q)
        for o in range(1, at.near_count):
            self.coming[o - 1].wait_recv()
            total += self.rx[o - 1].astype(F32)
        self.fz[at.zh] = total.astype(BF16)
        self.coming = [self.go(self.fz.at[at.zh], self.fz.at[at.zh], at.far(o)) for o in range(1, at.far_count)]

    def back_near(self):
        at = self.at
        for copy in self.coming:
            copy.wait_recv()
        total = self.fz[0].astype(F32)
        for k in range(1, at.far_count):
            total += self.fz[k].astype(F32)
        mine = self.rows(at.q)
        self.out[mine, :] = total.astype(BF16)
        src = self.out.at[mine]
        self.coming = [self.go(src, src, at.near(o)) for o in range(1, at.near_count)]
        self.crossing = [self.go(src, src, at.core())]

    def back_core(self):
        at = self.at
        for o in range(1, at.near_count):
            self.coming[o - 1].wait_recv()
            src = self.out.at[self.rows(at.q - o + at.near_count)]
            self.crossing.append(self.go(src, src, at.core()))

    def finish(self):
        for copy in self.crossing:
            copy.wait_recv()
        for copy in self.sent:
            copy.wait_send()


def kernel(
    at,
    tok_hbm, og_hbm, b_hbm, c_hbm, glu_hbm, len_hbm, gain_hbm, skip_hbm, nu_hbm, theta_hbm, gam_hbm,
    block_ref, ing_ref, grads_ref, small_ref,
    tok, og, bw, cw, gw, bout, xhat, rstd, u, x, h, hl, dg, g, dz, dy, dh, order, back_order,
    edge, init, msg, rmsg, part, rc, sc, rx, fz, smc, smn, smf,
    len_ref, gain_ref, skip_ref, nu_ref, theta_ref, gam_ref,
    load_sem, msend, mrecv, asend, arecv, ssend, srecv,
):
    at.here()
    seq = at.seq
    tokens, width = tok.shape
    chan = width // 2
    tiles = tokens // TILE
    blocks = tiles * SUB
    lo, hi = slice(0, chan), slice(chan, width)

    def tile_rows(i):
        return pl.ds(pl.multiple_of(i * TILE, TILE), TILE)

    loads = []

    def load(src, dst):
        copy = pltpu.make_async_copy(src, dst, load_sem.at[len(loads)])
        copy.start()
        loads.append(copy)
        return copy

    def tok_in(i):
        return pltpu.make_async_copy(tok_hbm.at[0, tile_rows(i)], tok.at[tile_rows(i)], load_sem.at[i])

    for i in range(tiles):
        tok_in(i).start()
        loads.append(None)
    vectors = [
        load(src, dst)
        for src, dst in (
            (nu_hbm, nu_ref), (theta_hbm, theta_ref), (gam_hbm, gam_ref), (gain_hbm, gain_ref),
            (skip_hbm, skip_ref), (len_hbm, len_ref),
        )
    ]
    b_in = [load(b_hbm.at[k], bw.at[:, pl.ds(k * chan, chan)]) for k in range(2)]
    c_in = [load(c_hbm.at[k], cw.at[pl.ds(k * chan, chan)]) for k in range(2)]
    glu_in = load(glu_hbm, gw)
    og_in = load(og_hbm.at[0], og)

    barrier = pltpu.get_barrier_semaphore()
    peers = at.peers()
    for peer in peers:
        pl.semaphore_signal(barrier, inc=1, device_id=peer, device_id_type=MESH)

    first = lax.broadcasted_iota(jnp.int32, (TILE, TILE), 0)
    second = lax.broadcasted_iota(jnp.int32, (TILE, TILE), 1)
    order[...] = (second == (first % SUB) * STEPS + first // SUB).astype(F32).astype(BF16)
    back_order[...] = (first == (second % SUB) * STEPS + second // SUB).astype(F32).astype(BF16)

    for copy in vectors:
        copy.wait()
    modulus = jnp.exp(-jnp.exp(nu_ref[...]))
    angle = jnp.exp(theta_ref[...])
    lam = (modulus * jnp.cos(angle), modulus * jnp.sin(angle))
    conj = (lam[0], -lam[1])
    lam_step = cpow2(lam, int(math.log2(STEPS)))
    lam_all = cpow2(lam_step, int(math.log2(blocks)))
    conj_step, conj_all = (lam_step[0], -lam_step[1]), (lam_all[0], -lam_all[1])
    scaling = jnp.exp(gam_ref[...])
    scale2 = jnp.concatenate([scaling, -scaling], axis=1)

    starts, total = [], jnp.int32(0)
    for k in range(len_ref.shape[1]):
        starts.append(total)
        total = total + len_ref[0, k]

    def keep_at(position):
        hit = functools.reduce(jnp.logical_or, [position == start for start in starts])
        return jnp.where(hit, 0.0, 1.0).astype(F32)

    def keep_all(device):
        begin = device * tokens
        hits = [jnp.logical_and(start >= begin, start < begin + tokens) for start in starts]
        return jnp.where(functools.reduce(jnp.logical_or, hits), 0.0, 1.0).astype(F32)

    tile_keep = [keep_at(at.s * tokens + i * TILE) for i in range(tiles)]

    def kept(k, value):
        if k % SUB:
            return value
        return value[0] * tile_keep[k // SUB], value[1] * tile_keep[k // SUB]

    gain = gain_ref[...]
    skip = skip_ref[...]
    for copy in b_in:
        copy.wait()

    def front(i, carry):
        rows = tile_rows(i)
        tok_in(i).wait()
        value = mm(order[...], tok[rows, :])
        tok[rows, :] = value.astype(BF16)
        centered = value - jnp.mean(value, axis=1, keepdims=True)
        inv = lax.rsqrt(jnp.mean(centered * centered, axis=1, keepdims=True) + EPS)
        normal = centered * inv
        xhat[rows, :] = normal
        rstd[rows, :] = inv
        low = (normal * gain).astype(BF16)
        u[rows, :] = low
        x[rows, :] = mm(low, bw[...]).astype(BF16).astype(F32) * scale2
        return carry

    lax.fori_loop(0, tiles, front, 0)

    def at_step(i, j, count=SUB):
        return pl.ds(pl.multiple_of(i * TILE + j * SUB, count), count)

    def pick(ref, i, j):
        rows = at_step(i, j)
        return ref[rows, lo], ref[rows, hi]

    def pick_tile(ref, i):
        return ref[i * SUB : (i + 1) * SUB, lo], ref[i * SUB : (i + 1) * SUB, hi]

    def both(value):
        return jnp.concatenate(value, axis=1)

    nothing = (jnp.zeros((SUB, chan), F32),) * 2
    zero_row = (jnp.zeros((1, chan), F32),) * 2

    def advance(j, carry):
        return [add(cmul(conj, carry[i]), pick(x, i, j)) for i in range(tiles)]

    def keep_edges(values):
        for i in range(tiles):
            edge[i * SUB : (i + 1) * SUB, :] = both(values[i])

    keep_edges(lax.fori_loop(0, STEPS, advance, [nothing] * tiles, unroll=4))

    def edge_row(k):
        return edge[k : k + 1, lo], edge[k : k + 1, hi]

    state = zero_row
    for k in range(blocks):
        state = add(edge_row(k), cmul(conj_step, kept(k, state)))

    def exchange(which, value):
        msg[which] = both(value)
        copies = []
        for o in range(seq - 1, 0, -1):
            copy = remote(
                msg.at[which], rmsg.at[which, o], msend.at[which, o], mrecv.at[which, o], at.group(o)
            )
            copy.start()
            copies.append(copy)
        return copies

    def gather(which, factor, copies, ahead):
        for copy in copies:
            copy.wait_recv()
        result = zero_row
        for o in range(seq - 1, 0, -1):
            source = at.s + o if ahead else at.s - o
            slot = seq - o if ahead else o
            there = (rmsg[which, slot, :, lo], rmsg[which, slot, :, hi])
            k = keep_all(source)
            new = add(there, cmul((factor[0] * k, factor[1] * k), result))
            valid = source < seq if ahead else source >= 0
            result = tuple(jnp.where(valid, a, b) for a, b in zip(new, result))
        return result

    pl.semaphore_wait(barrier, len(peers))
    sent_forward = exchange(0, state)
    carry = gather(0, conj_all, sent_forward, False)

    for k in range(blocks):
        begin = kept(k, carry)
        init[k : k + 1, :] = both(begin)
        if k + 1 < blocks:
            carry = add(edge_row(k), cmul(conj_step, begin))

    def advance_store(pair, carry):
        states = [[], []]
        for n in range(2):
            carry = advance(pair * 2 + n, carry)
            states[n] = [both(value) for value in carry]
        for i in range(tiles):
            rows = at_step(i, pair * 2, 2 * SUB)
            value = jnp.concatenate([states[0][i], states[1][i]], axis=0)
            h[rows, :] = value
            hl[rows, :] = value.astype(BF16)
        return carry

    lax.fori_loop(0, STEPS // 2, advance_store, [pick_tile(init, i) for i in range(tiles)], unroll=2)

    for copy in c_in:
        copy.wait()
    glu_in.wait()
    og_in.wait()

    def middle(i, skip_sum):
        rows = tile_rows(i)
        ul = u[rows, :].astype(F32)
        v = mm(hl[rows, :], cw[...]) + skip * ul
        square = v * v
        t = jnp.tanh(v * (0.7978845608028654 + 0.7978845608028654 * 0.044715 * square))
        half = 0.5 + 0.5 * t
        wide = v * half
        slope = half + wide * (1.0 - half) * (2 * 0.7978845608028654 + 6 * 0.7978845608028654 * 0.044715 * square)
        gl = wide.astype(BF16)
        g[rows, :] = gl
        value = mm(gl, gw[:, :width])
        s = 0.5 + 0.5 * jnp.tanh(0.5 * mm(gl, gw[:, width:]))
        branch = value * s
        bout[rows, :] = (tok[rows, :].astype(F32) + branch).astype(BF16)
        cot = mm(order[...], og[rows, :])
        og[rows, :] = cot.astype(BF16)
        scaled = cot * s
        dvalue = scaled.astype(BF16)
        dgate = (scaled * (value - branch)).astype(BF16)
        dz[rows, :width] = dvalue
        dz[rows, width:] = dgate
        back = mm(dvalue, gw[:, :width], NT) + mm(dgate, gw[:, width:], NT)
        dyl = (back * slope).astype(BF16)
        dy[rows, :] = dyl
        dh[rows, :] = mm(dyl, cw[...], NT).astype(BF16).astype(F32)
        return skip_sum + fold(dyl.astype(F32) * ul)

    skip_sum = lax.fori_loop(0, tiles, middle, jnp.zeros((8, width), F32))

    def retreat(k, carry):
        j = STEPS - 1 - k
        return [cmul(lam, add(pick(dh, i, j), carry[i])) for i in range(tiles)]

    keep_edges(lax.fori_loop(0, STEPS, retreat, [nothing] * tiles, unroll=4))
    state = zero_row
    for k in range(blocks - 1, -1, -1):
        state = kept(k, add(edge_row(k), cmul(lam_step, state)))
    sent_backward = exchange(1, state)

    sums = [
        Sum(
            at, part.at[k], grads_ref.at[k], rc.at[k], sc.at[k], rx.at[k], fz.at[k], asend.at[k], arecv.at[k]
        )
        for k in range(4)
    ]
    sums[0].start_core(g, dz.at[:, pl.ds(0, width)])
    sums[1].start_core(g, dz.at[:, pl.ds(width, width)])
    sums[0].start_near()
    sums[2].start_core(hl, dy)
    sums[1].start_near()

    incoming = gather(1, lam_all, sent_backward, True)
    for k in range(blocks - 1, -1, -1):
        if k > 0:
            following = kept(k, add(edge_row(k), cmul(lam_step, incoming)))
        edge[k : k + 1, :] = both(incoming)
        if k > 0:
            incoming = following

    def adjoint(j, carry, before):
        states, sums_of = carry
        pre, pim, gsum = sums_of
        result, grads = [], []
        for i in range(tiles):
            wre, wim = add(pick(dh, i, j), states[i])
            yre, yim = before[i]
            xre, xim = pick(x, i, j)
            pre = pre + (yre * wre + yim * wim)
            pim = pim + (yim * wre - yre * wim)
            gsum = gsum + (xre * wre + xim * wim)
            grads.append(both((scaling * wre, -scaling * wim)))
            result.append(cmul(lam, (wre, wim)))
        return (result, (pre, pim, gsum)), grads

    def put_pair(pair, early, late):
        for i in range(tiles):
            dg[at_step(i, pair * 2, 2 * SUB), :] = jnp.concatenate([early[i], late[i]], axis=0).astype(BF16)

    def before_of(j):
        return [pick(h, i, j - 1) for i in range(tiles)]

    def adjoint_pair(k, carry):
        pair = STEPS // 2 - 1 - k
        carry, late = adjoint(pair * 2 + 1, carry, before_of(pair * 2 + 1))
        carry, early = adjoint(pair * 2, carry, before_of(pair * 2))
        put_pair(pair, early, late)
        return carry

    carry = ([pick_tile(edge, i) for i in range(tiles)], (jnp.zeros((SUB, chan), F32),) * 3)
    carry = lax.fori_loop(0, STEPS // 2 - 1, adjoint_pair, carry)
    carry, late = adjoint(1, carry, before_of(1))
    carry, early = adjoint(0, carry, [pick_tile(init, i) for i in range(tiles)])
    put_pair(0, early, late)
    pre, pim, gsum = (jnp.sum(value, axis=0, keepdims=True) for value in carry[1])

    sums[3].start_core(u, dg)

    def put_block(i, carry):
        block_ref[0, tile_rows(i), :] = mm(back_order[...], bout[tile_rows(i), :]).astype(BF16)
        return carry

    lax.fori_loop(0, tiles, put_block, 0)
    sums[3].start_near()
    sums[2].start_near()

    def last_tile(i, gain_sum):
        rows = tile_rows(i)
        du = mm(dg[rows, :], bw[...], NT) + skip * dy[rows, :].astype(F32)
        normal = xhat[rows, :]
        e = gain * du
        mean_e = jnp.mean(e, axis=1, keepdims=True)
        mean_ex = jnp.mean(e * normal, axis=1, keepdims=True)
        grad = og[rows, :].astype(F32) + (e - mean_e - normal * mean_ex) * rstd[rows, :]
        ing_ref[0, rows, :] = mm(back_order[...], grad.astype(BF16)).astype(BF16)
        return gain_sum + fold(du * normal)

    gain_sum = lax.fori_loop(0, tiles, last_tile, jnp.zeros((8, width), F32))

    small = [
        jnp.sum(gain_sum, axis=0, keepdims=True),
        jnp.sum(skip_sum, axis=0, keepdims=True),
        -jnp.exp(nu_ref[...]) * (lam[0] * pre + lam[1] * pim),
        angle * (lam[0] * pim - lam[1] * pre),
        gsum,
    ]
    row = 0
    for value in small:
        for k in range(value.shape[1] // LANES):
            smc[at.c, row : row + 1, :] = value[:, k * LANES : (k + 1) * LANES]
            row += 1
    smc[at.c, row:, :] = jnp.zeros((smc.shape[1] - row, LANES), F32)
    small_slot = 0
    small_sent = []

    def spread(buffer, index, targets):
        nonlocal small_slot
        copies = []
        for target in targets:
            copy = remote(buffer.at[index], buffer.at[index], ssend.at[small_slot], srecv.at[small_slot], target)
            small_slot += 1
            copy.start()
            copies.append(copy)
        small_sent.extend(copies)
        return copies

    def collect(buffer, count, copies):
        for copy in copies:
            copy.wait_recv()
        value = buffer[0]
        for k in range(1, count):
            value = value + buffer[k]
        return value

    copies = spread(smc, at.c, [at.core()])
    sums[0].start_far()
    sums[1].start_far()
    smn[at.q] = collect(smc, 2, copies)
    copies = spread(smn, at.q, [at.near(o) for o in range(1, at.near_count)])
    sums[3].start_far()
    sums[2].start_far()
    sums[0].back_near()
    sums[1].back_near()
    smf[at.zh] = collect(smn, at.near_count, copies)
    copies = spread(smf, at.zh, [at.far(o) for o in range(1, at.far_count)])
    sums[3].back_near()
    sums[2].back_near()
    for k in (0, 1, 3, 2):
        sums[k].back_core()
    small_ref[...] = collect(smf, at.far_count, copies)
    for one in sums:
        one.finish()
    for copy in sent_forward + sent_backward + small_sent:
        copy.wait_send()


def finish(
    block_in, ing_in, grads, small, block_out, in_grad, b_grad, c_grad, glu_grad, gain, skip, nu, theta, gamma,
    wide, sem,
):
    rows, chan = grads.shape[1], b_grad.shape[2]
    copies = []

    def store(src, dst):
        copy = pltpu.make_async_copy(src, dst, sem.at[len(copies)])
        copy.start()
        copies.append(copy)

    store(block_in, block_out)
    store(ing_in, in_grad)
    for k, targets in enumerate((
        [(slice(None), glu_grad.at[:, pl.ds(0, rows)])],
        [(slice(None), glu_grad.at[:, pl.ds(rows, rows)])],
        [(slice(0, chan), c_grad.at[0]), (slice(chan, rows), c_grad.at[1])],
    )):
        wide[k] = grads[k].astype(F32)
        for part, target in targets:
            store(wide.at[k, part], target)
    wide[3] = grads[3].astype(F32)
    for k in range(2):
        store(wide.at[3, :, pl.ds(k * chan, chan)], b_grad.at[k])
    row = 0
    for ref in (gain, skip, nu, theta, gamma):
        ref[...] = small[row : row + ref.shape[0], :]
        row += ref.shape[0]
    for copy in copies:
        copy.wait()


def on_device(seq, dp, tokens, lengths, gain, b_proj, c_proj, skip, nu, theta, gamma_log, glu, out_grad):
    _, count, width = tokens.shape
    chan = nu.shape[0]
    at = Place(seq, dp)
    piece = ROWS // 2 // at.near_count
    slots = 1 + 3 * at.near_count - 2 + at.far_count - 1
    small_slots = 1 + (at.near_count - 1) + (at.far_count - 1)
    blocks = count // STEPS
    anywhere = pl.BlockSpec(memory_space=pl.ANY)
    vmem = pl.BlockSpec(memory_space=pltpu.VMEM)
    dma = pltpu.SemaphoreType.DMA
    wide, low = pltpu.VMEM((count, width), F32), pltpu.VMEM((count, width), BF16)
    block, ing, grads, small = pl.pallas_call(
        functools.partial(kernel, at),
        out_shape=(
            pltpu.VMEM(tokens.shape, BF16),
            pltpu.VMEM(tokens.shape, BF16),
            pltpu.VMEM((4, ROWS, ROWS), BF16),
            pltpu.VMEM((16, LANES), F32),
        ),
        in_specs=[anywhere] * 11,
        out_specs=(vmem,) * 4,
        scratch_shapes=[
            low, low,
            pltpu.VMEM((width, 2 * chan), BF16),
            pltpu.VMEM((2 * chan, width), BF16),
            pltpu.VMEM((width, 2 * width), BF16),
            low,
            wide,
            pltpu.VMEM((count, 1), F32),
            low,
            wide, wide,
            low, low, low,
            pltpu.VMEM((count, 2 * width), BF16),
            low,
            wide,
            pltpu.VMEM((TILE, TILE), BF16),
            pltpu.VMEM((TILE, TILE), BF16),
            pltpu.VMEM((blocks, 2 * chan), F32),
            pltpu.VMEM((blocks, 2 * chan), F32),
            pltpu.VMEM((2, 1, 2 * chan), F32),
            pltpu.VMEM((2, seq, 1, 2 * chan), F32),
            pltpu.VMEM((4, ROWS, ROWS), BF16),
            pltpu.VMEM((4, ROWS // 2, ROWS), BF16),
            pltpu.VMEM((4, at.near_count - 1, piece, ROWS), BF16),
            pltpu.VMEM((4, at.near_count - 1, piece, ROWS), BF16),
            pltpu.VMEM((4, at.far_count, piece, ROWS), BF16),
            pltpu.VMEM((2, 16, LANES), F32),
            pltpu.VMEM((at.near_count, 16, LANES), F32),
            pltpu.VMEM((at.far_count, 16, LANES), F32),
            pltpu.SMEM(lengths.shape, jnp.int32),
            pltpu.VMEM((1, width), F32),
            pltpu.VMEM((1, width), F32),
            pltpu.VMEM((1, chan), F32),
            pltpu.VMEM((1, chan), F32),
            pltpu.VMEM((1, chan), F32),
            dma((count // TILE + 12,)),
            dma((2, seq)),
            dma((2, seq)),
            dma((4, slots)),
            dma((4, slots)),
            dma((small_slots,)),
            dma((small_slots,)),
        ],
        compiler_params=pltpu.CompilerParams(
            collective_id=0, has_side_effects=True, vmem_limit_bytes=40 * 2**20
        ),
    )(
        *(
            pltpu.with_memory_space_constraint(value, pltpu.HBM)
            for value in (
                tokens, out_grad, b_proj, c_proj, glu, lengths,
                gain[None], skip[None], nu[None], theta[None], gamma_log[None],
            )
        )
    )
    lines = [(k, LANES) for k in (width // LANES,) * 2 + (chan // LANES,) * 3]
    block_out, in_grad, b_grad, c_grad, glu_grad, *rest = pl.pallas_call(
        finish,
        out_shape=(
            jax.ShapeDtypeStruct(tokens.shape, BF16),
            jax.ShapeDtypeStruct(tokens.shape, BF16),
            jax.ShapeDtypeStruct(b_proj.shape, F32),
            jax.ShapeDtypeStruct(c_proj.shape, F32),
            jax.ShapeDtypeStruct(glu.shape, F32),
        ) + tuple(jax.ShapeDtypeStruct(line, F32) for line in lines),
        in_specs=[vmem] * 4,
        out_specs=(anywhere,) * 5 + (vmem,) * 5,
        scratch_shapes=[pltpu.VMEM((4, ROWS, ROWS), F32), dma((8,))],
        compiler_params=pltpu.CompilerParams(vmem_limit_bytes=16 * 2**20),
    )(block, ing, grads, small)
    gain_grad, skip_grad, nu_grad, theta_grad, gamma_grad = (value.reshape(-1) for value in rest)
    return (
        block_out, in_grad, gain_grad, b_grad, c_grad, skip_grad, nu_grad, theta_grad, gamma_grad, glu_grad,
    )


def solution(mesh):
    rows, whole = P("dp", "seq", None), P()
    return jax.shard_map(
        functools.partial(on_device, mesh.shape["seq"], mesh.shape["dp"]),
        mesh=mesh,
        in_specs=(rows, P("dp", None)) + (whole,) * 8 + (rows,),
        out_specs=(rows, rows) + (whole,) * 8,
        check_vma=False,
    )
```

time: 80.7 us -> 56.8 us (0.70)
  Pallas kernels: 68.8 us -> 56 us
  local copies, waits for them, and re-layouts: 7.73 us -> 0 us
  other arithmetic: 3.07 us -> 0 us
    pallas_call x1 -> x2, Pallas kernels: 68.8 us -> 56 us  [the longest x1 52.7 us: on_device(): pl.pallas_call(functools.partial(kernel, at), out_shape=(pltpu.VMEM(token...]
    slice x3 -> x0, local copies, waits for them, and re-layouts: 4.97 us -> none  [the longest x1 2.14 us: on_device(): c_grad = grads[2].reshape(2, chan, width)]
    unnamed x8 -> x0, local copies, waits for them, and re-layouts: 2.37 us -> none
    concatenate x1 -> x0, other arithmetic: 1.46 us -> none  [on_device(): glu_grad = jnp.concatenate([grads[0], grads[1]], axis=1)]
    another operation x1 -> x0, other arithmetic: 1.04 us -> none  [on_device(): b_grad = jnp.stack([grads[3][:, :chan], grads[3][:, chan:]])]
where the time goes in v1:
time: 56.8 us; the launch traced here: 56.7 us
  Pallas kernels  56 us (99%)
  between operations  0.65 us (1%)
    pallas_call x1, Pallas kernels, on_device(): pl.pallas_call(functools.partial(kernel, at), out_shape=(pltpu.VMEM(token...  52.7 us
    pallas_call x1, Pallas kernels, on_device(): pl.pallas_call(finish, out_shape=(jax.ShapeDtypeStruct(tokens.shape, BF16...  3.31 us

profile of v1, /device:TPU:0, one launch (start us, length us, event | category | flops | bytes accessed | tf_op | source)
XLA Modules:
  0.0 56.7 jit_solution(14626904284731605781)
XLA Ops:
  0.6 52.7 %shard_map.186 = (bf16[1,1024,512]{2,1,0:T(8,128)(2,1)S(1)}, bf16[1,1024,512]{2,1,0:T(8,128)(2,1)S(1)}, bf16[4,512,512]{2,1,0:T(8,128)(2,1)S(1)}, f32[16,128]{1,0:T(8,128)S(1)}) custom-call(bf16[1,1024,512]{2,1,0:T(8,128)(2,1)} %tok_hbm.1, bf16[1,1024,512]{2,1,0:T(8,128)(2,1)} %og_hbm.1, bf16[2,512,256]{2,1,0:T(8,128)(2,1)} %b_hbm.1, ...), custom_call_target="tpu_custom_call" | custom-call | tf_op jit(solution)/shard_map/pallas_call | solution.py:597
  53.4 3.3 %shard_map.187 = (bf16[1,1024,512]{2,1,0:T(8,128)(2,1)}, bf16[1,1024,512]{2,1,0:T(8,128)(2,1)}, f32[2,512,256]{2,1,0:T(8,128)}, f32[2,256,512]{2,1,0:T(8,128)}, ...) custom-call(bf16[1,1024,512]{2,1,0:T(8,128)(2,1)S(1)} %get-tuple-ele, ...), custom_call_target="tpu_custom_call" | custom-call | tf_op jit(solution)/shard_map/pallas_call | solution.py:662

commit v2 on v1

v2 whole, which is shorter than its diff:
```python
import functools
import math

import jax
import jax.numpy as jnp
from jax import lax
from jax.experimental import pallas as pl
from jax.experimental.pallas import tpu as pltpu
from jax.sharding import PartitionSpec as P

MESH = pl.DeviceIdType.MESH
F32, BF16 = jnp.float32, jnp.bfloat16
EPS = 1e-5
TILE = 256
LANES = 128
SUB = 8
STEPS = TILE // SUB
ROWS = 512
NT = (((1,), (1,)), ((), ()))
TN = (((0,), (0,)), ((), ()))


def mm(a, b, dims=(((1,), (0,)), ((), ()))):
    return lax.dot_general(a, b, dims, preferred_element_type=F32)


def add(a, b):
    return a[0] + b[0], a[1] + b[1]


def cmul(a, b):
    return a[0] * b[0] - a[1] * b[1], a[0] * b[1] + a[1] * b[0]


def cpow2(a, times):
    for _ in range(times):
        a = cmul(a, a)
    return a


def fold(value):
    return jnp.sum(value.reshape(-1, 8, value.shape[1]), axis=0)


class Place:
    def __init__(self, seq, dp):
        self.seq, self.dp = seq, dp
        self.nx = max(1, math.isqrt(seq // 2))
        self.nz = seq // self.nx
        self.ny = dp // 2
        plane = self.nx * self.ny
        self.zl = 2 if self.nz % 2 == 0 and (ROWS // 2 // (2 * plane)) % 16 == 0 else 1
        self.near_count, self.far_count = self.zl * plane, self.nz // self.zl
        self.sizes = (self.zl, self.nx, self.ny)

    def here(self):
        self.s, self.d = lax.axis_index("seq"), lax.axis_index("dp")
        self.z, self.x = self.s // self.nx, lax.rem(self.s, self.nx)
        self.y, self.c = self.d // 2, lax.rem(self.d, 2)
        self.zh, self.zo = self.z // self.zl, lax.rem(self.z, self.zl)
        self.q = (self.zo * self.nx + self.x) * self.ny + self.y
        self.inner = (self.zo, self.x, self.y)
        return self

    def member(self, inner):
        return ((self.zh * self.zl + inner[0]) * self.nx + inner[1], inner[2] * 2 + self.c)

    def core(self):
        return (self.s, self.y * 2 + 1 - self.c)

    def near(self, o):
        q = lax.rem(self.q + o, self.near_count)
        return self.member((q // (self.nx * self.ny), lax.rem(q // self.ny, self.nx), lax.rem(q, self.ny)))

    def far(self, o):
        zh = lax.rem(self.zh + o, self.far_count)
        return ((zh * self.zl + self.zo) * self.nx + self.x, self.d)

    def group(self, o):
        return (lax.rem(self.s + o, self.seq), self.d)

    def peers(self):
        found = [self.core()] + [self.group(o) for o in range(1, self.seq)]
        for oy in range(1, self.ny):
            y = lax.rem(self.y + oy, self.ny)
            for zo in range(self.zl):
                for x in range(self.nx):
                    found.append(((self.zh * self.zl + zo) * self.nx + x, y * 2 + self.c))
        return found


def remote(src, dst, send, recv, device):
    copy = pltpu.make_async_remote_copy(
        src_ref=src, dst_ref=dst, send_sem=send, recv_sem=recv, device_id=device, device_id_type=MESH
    )
    copy.start()


def take(ref, sem):
    pltpu.make_async_copy(ref, ref, sem).wait()


class Sum:
    @staticmethod
    def scratch(at, width, first, last):
        half, piece = ROWS // 2, ROWS // 2 // at.near_count
        count = at.near_count // (1 if first is None else at.sizes[first])
        dma = pltpu.SemaphoreType.DMA
        shapes = [(half, width), (count - 1, piece, width), (count - 1, piece, width), (at.far_count, piece, width)]
        if first is not None:
            shapes += [(half // 2, width), (half // 2, width)]
        return [pltpu.VMEM(shape, BF16) for shape in shapes] + [
            dma((1,)), dma((5 + (first is not None) + 2 * (last is not None),))
        ]

    def __init__(self, at, first, last, out, part, rc, sc, rx, fz, *rest):
        self.at, self.first, self.last, self.out, self.part = at, first, last, out, part
        self.rc, self.sc, self.rx, self.fz = rc, sc, rx, fz
        self.send, self.recv = rest[-2:]
        if first is not None:
            self.s1, self.r1 = rest[:2]
        self.sent = 0
        self.half = ROWS // 2
        self.piece = self.half // at.near_count
        self.row0 = pl.multiple_of(at.c * self.half, 16)
        self.major = first if first is not None else last if last is not None else 0
        self.axes = [self.major] + [k for k in range(3) if k != self.major]
        self.rest = math.prod(at.sizes[k] for k in self.axes[1:])
        self.me = 0
        for k in self.axes:
            self.me = self.me * at.sizes[k] + at.inner[k]
        self.base = at.inner[self.major] * self.rest

    def others(self, axis):
        at = self.at
        count = at.near_count if axis is None else self.rest
        first = 0 if axis is None else self.base
        for o in range(1, count):
            place = first + lax.rem(self.me - first + o, count)
            inner, left = [None] * 3, place
            for k in reversed(self.axes):
                inner[k] = lax.rem(left, at.sizes[k])
                left = left // at.sizes[k]
            yield at.member(inner), place

    def mirror(self):
        inner = list(self.at.inner)
        inner[self.major] = 1 - inner[self.major]
        return self.at.member(inner)

    def go(self, slot, src, dst, device):
        remote(src, dst, self.send.at[0], self.recv.at[slot], device)
        self.sent += math.prod(src.shape[:-1])

    def share(self, slot, src, device):
        self.go(slot, src, src, device)

    def drain(self):
        if self.sent:
            take(self.part.at[pl.ds(0, self.sent)], self.send.at[0])
        self.sent = 0

    def local(self, place, count=1):
        return pl.ds(pl.multiple_of(place * self.piece, 16), count * self.piece)

    def rows(self, place, count=1):
        return pl.ds(pl.multiple_of(self.row0 + place * self.piece, 16), count * self.piece)

    def theirs(self):
        return (1 - self.at.inner[self.major]) * self.rest

    def start_core(self):
        other = pl.ds(pl.multiple_of((1 - self.at.c) * self.half, self.half), self.half)
        self.go(0, self.part.at[other], self.rc, self.at.core())

    def both(self, place, count=1):
        mine = self.part[self.rows(place, count), :].astype(F32)
        return mine + self.rc[self.local(place, count), :].astype(F32)

    def start_axis(self):
        take(self.rc, self.recv.at[0])
        self.drain()
        if self.first is not None:
            self.s1[...] = self.both(self.theirs(), self.rest).astype(BF16)
            self.go(5, self.s1, self.r1, self.mirror())

    def held(self, place):
        value = self.both(place)
        if self.first is not None:
            value = value + self.r1[self.local(place - self.base), :].astype(F32)
        return value

    def start_near(self):
        if self.first is not None:
            take(self.r1, self.recv.at[5])
            self.drain()
        for o, (device, place) in enumerate(self.others(self.first)):
            self.sc[o] = self.held(place).astype(BF16)
            self.go(1, self.sc.at[o], self.rx.at[o], device)

    def start_far(self):
        at = self.at
        total = self.held(self.me)
        take(self.rx, self.recv.at[1])
        self.drain()
        for o in range(self.rx.shape[0]):
            total += self.rx[o].astype(F32)
        self.fz[at.zh] = total.astype(BF16)
        for o in range(1, at.far_count):
            self.share(2, self.fz.at[at.zh], at.far(o))

    def back_near(self):
        at = self.at
        if at.far_count > 1:
            take(self.fz.at[pl.ds(0, at.far_count - 1)], self.recv.at[2])
        self.drain()
        total = self.fz[0].astype(F32)
        for k in range(1, at.far_count):
            total += self.fz[k].astype(F32)
        mine = self.rows(self.me)
        self.out[mine, :] = total.astype(BF16)
        for device, _ in self.others(self.last):
            self.share(3, self.out.at[mine], device)

    def back_axis(self):
        count = self.at.near_count if self.last is None else self.rest
        take(self.out.at[pl.ds(0, (count - 1) * self.piece)], self.recv.at[3])
        self.drain()
        src = self.out.at[self.rows(0 if self.last is None else self.base, count)]
        if self.last is not None:
            self.share(self.recv.shape[0] - 2, src, self.mirror())
        self.share(4, src, self.at.core())

    def back_core(self):
        if self.last is not None:
            src = self.out.at[self.rows(self.theirs(), self.rest)]
            take(src, self.recv.at[self.recv.shape[0] - 2])
            self.drain()
            self.share(self.recv.shape[0] - 1, src, self.at.core())

    def finish(self):
        count = self.at.near_count if self.last is None else self.rest
        took = self.out.at[pl.ds(0, count * self.piece)]
        take(took, self.recv.at[4])
        if self.last is not None:
            take(took, self.recv.at[self.recv.shape[0] - 1])
        self.drain()


STAGES = {
    "a": "start_axis", "n": "start_near", "f": "start_far",
    "b": "back_near", "x": "back_axis", "c": "back_core", "e": "finish",
}


PLAN = (
    ("m01", "m23", "m45", "a0", "a1", "a2", "a3", "n3",),
    (),
    ("a4", "a5", "n5",),
    ("m67",),
    (),
    ("a6", "a7", "n0", "n1", "n2",),
    (
        "s0", "n4", "f3", "s1", "f5", "n6", "n7", "f0", "f1", "f2", "b3", "f4", "s2", "b5",
        "f6", "f7", "b0", "b1", "b2", "s3", "x3", "b4", "x5", "b6", "c3", "e3", "b7", "x0",
        "x1", "x2", "x4", "c0", "e0", "c5", "e5", "x6", "c1", "x7", "c2", "c6", "e6", "c4",
        "e1", "c7", "e7", "e2", "e4",
    ),
)
AXES = (
    (0, None), (1, 1), (2, 2), (None, None), (0, 0), (None, 0), (1, None), (0, None),
)


def unit_specs(at):
    return AXES if at.sizes == (2, 2, 2) else ((None, None),) * len(AXES)


def kernel(
    at,
    tok_hbm, og_hbm, b_hbm, c_hbm, glu_hbm, len_hbm, gain_hbm, skip_hbm, nu_hbm, theta_hbm, gam_hbm,
    block_ref, ing_ref, out_refs, small_ref,
    tok, og, bw, cw, gw, bout, xhat, rstd, u, x, h, hl, dg, ut, ht, gt, dz, dy, dh, order, back_order,
    edge, init, msg, rmsg, part, units, smc, smn, smf,
    len_ref, vectors,
    load_sem, msend, mrecv, ssend, srecv,
):
    at.here()
    seq = at.seq
    tokens, width = tok.shape
    chan = width // 2
    tiles = tokens // TILE
    blocks = tiles * SUB
    lo, hi = slice(0, chan), slice(chan, width)

    def tile_rows(i):
        return pl.ds(pl.multiple_of(i * TILE, TILE), TILE)

    barrier = pltpu.get_barrier_semaphore()
    peers = at.peers()
    for peer in peers:
        pl.semaphore_signal(barrier, inc=1, device_id=peer, device_id_type=MESH)

    def tok_in(i):
        return pltpu.make_async_copy(tok_hbm.at[0, tile_rows(i)], tok.at[tile_rows(i)], load_sem.at[6 + i])

    def load(src, dst, sem):
        pltpu.make_async_copy(src, dst, load_sem.at[sem]).start()

    vector_at, spans = 0, []
    for src in (nu_hbm, theta_hbm, gam_hbm, gain_hbm, skip_hbm):
        here = pl.ds(vector_at, src.shape[1])
        load(src, vectors.at[:, here], 0)
        spans.append(here)
        vector_at += src.shape[1]
    load(len_hbm, len_ref, 1)
    tok_in(0).start()
    for k in range(2):
        load(b_hbm.at[k], bw.at[:, pl.ds(k * chan, chan)], 2)
    for i in range(1, tiles):
        tok_in(i).start()
    for k in range(2):
        load(c_hbm.at[k], cw.at[pl.ds(k * chan, chan)], 3)
    load(glu_hbm, gw, 4)
    load(og_hbm.at[0], og, 5)

    first = lax.broadcasted_iota(jnp.int32, (TILE, TILE), 0)
    second = lax.broadcasted_iota(jnp.int32, (TILE, TILE), 1)
    order[...] = (second == (first % SUB) * STEPS + first // SUB).astype(F32).astype(BF16)
    back_order[...] = (first == (second % SUB) * STEPS + second // SUB).astype(F32).astype(BF16)

    take(vectors, load_sem.at[0])
    take(len_ref, load_sem.at[1])
    nu, theta, gamma, gain, skip = (vectors[:, here] for here in spans)
    modulus = jnp.exp(-jnp.exp(nu))
    angle = jnp.exp(theta)
    lam = (modulus * jnp.cos(angle), modulus * jnp.sin(angle))
    conj = (lam[0], -lam[1])
    lam_step = cpow2(lam, int(math.log2(STEPS)))
    lam_all = cpow2(lam_step, int(math.log2(blocks)))
    conj_step, conj_all = (lam_step[0], -lam_step[1]), (lam_all[0], -lam_all[1])
    scaling = jnp.exp(gamma)
    scale2 = jnp.concatenate([scaling, -scaling], axis=1)

    starts, total = [], jnp.int32(0)
    for k in range(len_ref.shape[1]):
        starts.append(total)
        total = total + len_ref[0, k]

    def keep_at(position):
        hit = functools.reduce(jnp.logical_or, [position == start for start in starts])
        return jnp.where(hit, 0.0, 1.0).astype(F32)

    def keep_all(device):
        begin = device * tokens
        hits = [jnp.logical_and(start >= begin, start < begin + tokens) for start in starts]
        return jnp.where(functools.reduce(jnp.logical_or, hits), 0.0, 1.0).astype(F32)

    tile_keep = [keep_at(at.s * tokens + i * TILE) for i in range(tiles)]

    def kept(k, value):
        if k % SUB:
            return value
        return value[0] * tile_keep[k // SUB], value[1] * tile_keep[k // SUB]

    take(bw, load_sem.at[2])

    def front(i, carry):
        rows = tile_rows(i)
        tok_in(i).wait()
        value = mm(order[...], tok[rows, :])
        tok[rows, :] = value.astype(BF16)
        centered = value - jnp.mean(value, axis=1, keepdims=True)
        inv = lax.rsqrt(jnp.mean(centered * centered, axis=1, keepdims=True) + EPS)
        normal = centered * inv
        xhat[rows, :] = normal
        rstd[rows, :] = inv
        low = (normal * gain).astype(BF16)
        u[rows, :] = low
        x[rows, :] = mm(low, bw[...]).astype(BF16).astype(F32) * scale2
        return carry

    lax.fori_loop(0, tiles, front, 0)

    def at_step(i, j, count=SUB):
        return pl.ds(pl.multiple_of(i * TILE + j * SUB, count), count)

    def pick(ref, i, j):
        rows = at_step(i, j)
        return ref[rows, lo], ref[rows, hi]

    def pick_tile(ref, i):
        return ref[i * SUB : (i + 1) * SUB, lo], ref[i * SUB : (i + 1) * SUB, hi]

    def both(value):
        return jnp.concatenate(value, axis=1)

    nothing = (jnp.zeros((SUB, chan), F32),) * 2
    zero_row = (jnp.zeros((1, chan), F32),) * 2

    def advance(j, carry):
        return [add(cmul(conj, carry[i]), pick(x, i, j)) for i in range(tiles)]

    def keep_edges(values):
        for i in range(tiles):
            edge[i * SUB : (i + 1) * SUB, :] = both(values[i])

    keep_edges(lax.fori_loop(0, STEPS, advance, [nothing] * tiles, unroll=4))

    def edge_row(k):
        return edge[k : k + 1, lo], edge[k : k + 1, hi]

    state = zero_row
    for k in range(blocks):
        state = add(edge_row(k), cmul(conj_step, kept(k, state)))

    others = pl.ds(1, seq - 1)

    def exchange(which, value):
        msg[which] = both(value)
        for o in range(seq - 1, 0, -1):
            remote(msg.at[which], rmsg.at[which, o], msend.at[which], mrecv.at[which], at.group(o))

    def gather(which, factor, ahead):
        take(rmsg.at[which, others], mrecv.at[which])
        result = zero_row
        for o in range(seq - 1, 0, -1):
            source = at.s + o if ahead else at.s - o
            slot = seq - o if ahead else o
            there = (rmsg[which, slot, :, lo], rmsg[which, slot, :, hi])
            k = keep_all(source)
            new = add(there, cmul((factor[0] * k, factor[1] * k), result))
            valid = source < seq if ahead else source >= 0
            result = tuple(jnp.where(valid, a, b) for a, b in zip(new, result))
        return result

    pl.semaphore_wait(barrier, len(peers))
    exchange(0, state)

    def turn_u(i, carry):
        ut[:, tile_rows(i)] = u[tile_rows(i), :].T
        return carry

    lax.fori_loop(0, tiles, turn_u, 0)
    carry = gather(0, conj_all, False)

    for k in range(blocks):
        begin = kept(k, carry)
        init[k : k + 1, :] = both(begin)
        if k + 1 < blocks:
            carry = add(edge_row(k), cmul(conj_step, begin))

    def advance_store(pair, carry):
        states = [[], []]
        for n in range(2):
            carry = advance(pair * 2 + n, carry)
            states[n] = [both(value) for value in carry]
        for i in range(tiles):
            rows = at_step(i, pair * 2, 2 * SUB)
            value = jnp.concatenate([states[0][i], states[1][i]], axis=0)
            h[rows, :] = value
            hl[rows, :] = value.astype(BF16)
        return carry

    lax.fori_loop(0, STEPS // 2, advance_store, [pick_tile(init, i) for i in range(tiles)], unroll=2)

    take(cw, load_sem.at[3])
    take(gw, load_sem.at[4])
    take(og, load_sem.at[5])

    def middle(i, skip_sum):
        rows = tile_rows(i)
        ul = u[rows, :].astype(F32)
        v = mm(hl[rows, :], cw[...]) + skip * ul
        square = v * v
        t = jnp.tanh(v * (0.7978845608028654 + 0.7978845608028654 * 0.044715 * square))
        half = 0.5 + 0.5 * t
        wide = v * half
        slope = half + wide * (1.0 - half) * (2 * 0.7978845608028654 + 6 * 0.7978845608028654 * 0.044715 * square)
        gl = wide.astype(BF16)
        gt[:, rows] = gl.T
        ht[:, rows] = hl[rows, :].T
        value = mm(gl, gw[:, :width])
        s = 0.5 + 0.5 * jnp.tanh(0.5 * mm(gl, gw[:, width:]))
        branch = value * s
        bout[rows, :] = (tok[rows, :].astype(F32) + branch).astype(BF16)
        cot = mm(order[...], og[rows, :])
        og[rows, :] = cot.astype(BF16)
        scaled = cot * s
        dvalue = scaled.astype(BF16)
        dgate = (scaled * (value - branch)).astype(BF16)
        dz[rows, :width] = dvalue
        dz[rows, width:] = dgate
        back = mm(dvalue, gw[:, :width], NT) + mm(dgate, gw[:, width:], NT)
        dyl = (back * slope).astype(BF16)
        dy[rows, :] = dyl
        dh[rows, :] = mm(dyl, cw[...], NT).astype(BF16).astype(F32)
        return skip_sum + fold(dyl.astype(F32) * ul)

    skip_sum = lax.fori_loop(0, tiles, middle, jnp.zeros((8, width), F32))

    def retreat(k, carry):
        j = STEPS - 1 - k
        return [cmul(lam, add(pick(dh, i, j), carry[i])) for i in range(tiles)]

    keep_edges(lax.fori_loop(0, STEPS, retreat, [nothing] * tiles, unroll=4))
    state = zero_row
    for k in range(blocks - 1, -1, -1):
        state = kept(k, add(edge_row(k), cmul(lam_step, state)))
    exchange(1, state)

    sums = [
        Sum(at, first, last, out, part.at[k], *refs)
        for k, ((first, last), out, refs) in enumerate(zip(unit_specs(at), out_refs, units))
    ]
    factors = [(gt, dz, 0), (gt, dz, 2), (ht, dy, 0), (ut, dg, 0)]

    def multiply(pair):
        left, right, column = factors[pair]
        half = ROWS // 2
        for core in (1 - at.c, at.c):
            rows = pl.ds(pl.multiple_of(core * half, half), half)

            def columns(n, carry, rows=rows):
                here = pl.ds(pl.multiple_of((column + n) * chan, chan), chan)
                part[2 * pair + n, rows, :] = mm(left[rows, :], right[:, here]).astype(BF16)
                return carry

            lax.fori_loop(0, 2, columns, 0)
            if core is not at.c:
                for n in range(2):
                    sums[2 * pair + n].start_core()

    def run(point):
        for step in PLAN[point]:
            if step[0] == "m":
                multiply(int(step[1]) // 2)
                continue
            for k in map(int, step[1:]):
                if step[0] == "s":
                    small_stage(k)
                else:
                    getattr(sums[k], STAGES[step[0]])()

    def spread(stage, buffer, index, targets):
        for target in targets:
            remote(buffer.at[index], buffer.at[index], ssend.at[stage], srecv.at[stage], target)

    def collect(stage, buffer):
        count = buffer.shape[0]
        if count > 1:
            take(buffer.at[pl.ds(0, count - 1)], srecv.at[stage])
            take(buffer.at[pl.ds(0, count - 1)], ssend.at[stage])
        value = buffer[0]
        for k in range(1, count):
            value = value + buffer[k]
        return value

    def small_stage(k):
        if k == 0:
            spread(0, smc, at.c, [at.core()])
        elif k == 1:
            smn[at.q] = collect(0, smc)
            spread(1, smn, at.q, [at.near(o) for o in range(1, at.near_count)])
        elif k == 2:
            smf[at.zh] = collect(1, smn)
            spread(2, smf, at.zh, [at.far(o) for o in range(1, at.far_count)])
        else:
            small_ref[...] = collect(2, smf)

    run(0)

    incoming = gather(1, lam_all, True)
    run(1)
    for k in range(blocks - 1, -1, -1):
        if k > 0:
            following = kept(k, add(edge_row(k), cmul(lam_step, incoming)))
        edge[k : k + 1, :] = both(incoming)
        if k > 0:
            incoming = following

    def adjoint(j, carry, before):
        states, sums_of = carry
        pre, pim, gsum = sums_of
        result, grads = [], []
        for i in range(tiles):
            wre, wim = add(pick(dh, i, j), states[i])
            yre, yim = before[i]
            xre, xim = pick(x, i, j)
            pre = pre + (yre * wre + yim * wim)
            pim = pim + (yim * wre - yre * wim)
            gsum = gsum + (xre * wre + xim * wim)
            grads.append(both((scaling * wre, -scaling * wim)))
            result.append(cmul(lam, (wre, wim)))
        return (result, (pre, pim, gsum)), grads

    def put_pair(pair, early, late):
        for i in range(tiles):
            dg[at_step(i, pair * 2, 2 * SUB), :] = jnp.concatenate([early[i], late[i]], axis=0).astype(BF16)

    def before_of(j):
        return [pick(h, i, j - 1) for i in range(tiles)]

    def adjoint_pair(k, carry):
        pair = STEPS // 2 - 1 - k
        carry, late = adjoint(pair * 2 + 1, carry, before_of(pair * 2 + 1))
        carry, early = adjoint(pair * 2, carry, before_of(pair * 2))
        put_pair(pair, early, late)
        return carry

    carry = ([pick_tile(edge, i) for i in range(tiles)], (jnp.zeros((SUB, chan), F32),) * 3)
    carry = lax.fori_loop(0, STEPS // 2 - 1, adjoint_pair, carry)
    carry, late = adjoint(1, carry, before_of(1))
    carry, early = adjoint(0, carry, [pick_tile(init, i) for i in range(tiles)])
    put_pair(0, early, late)
    pre, pim, gsum = (jnp.sum(value, axis=0, keepdims=True) for value in carry[1])

    run(2)
    run(3)

    def put_block(i, carry):
        block_ref[0, tile_rows(i), :] = mm(back_order[...], bout[tile_rows(i), :]).astype(BF16)
        return carry

    lax.fori_loop(0, tiles, put_block, 0)
    run(4)

    def last_tile(i, gain_sum):
        rows = tile_rows(i)
        du = mm(dg[rows, :], bw[...], NT) + skip * dy[rows, :].astype(F32)
        normal = xhat[rows, :]
        e = gain * du
        mean_e = jnp.mean(e, axis=1, keepdims=True)
        mean_ex = jnp.mean(e * normal, axis=1, keepdims=True)
        grad = og[rows, :].astype(F32) + (e - mean_e - normal * mean_ex) * rstd[rows, :]
        ing_ref[0, rows, :] = mm(back_order[...], grad.astype(BF16)).astype(BF16)
        return gain_sum + fold(du * normal)

    gain_sum = lax.fori_loop(0, tiles // 2, last_tile, jnp.zeros((8, width), F32))
    run(5)
    gain_sum = lax.fori_loop(tiles // 2, tiles, last_tile, gain_sum)

    small = [
        jnp.sum(gain_sum, axis=0, keepdims=True),
        jnp.sum(skip_sum, axis=0, keepdims=True),
        -jnp.exp(nu) * (lam[0] * pre + lam[1] * pim),
        angle * (lam[0] * pim - lam[1] * pre),
        gsum,
    ]
    row = 0
    for value in small:
        for k in range(value.shape[1] // LANES):
            smc[at.c, row : row + 1, :] = value[:, k * LANES : (k + 1) * LANES]
            row += 1
    smc[at.c, row:, :] = jnp.zeros((smc.shape[1] - row, LANES), F32)

    run(6)
    for which in range(2):
        take(rmsg.at[which, others], msend.at[which])


def finish(
    block_in, ing_in, sums, small,
    block_out, in_grad, b_grad, c_grad, glu_grad, gain, skip, nu, theta, gamma, wide, sem,
):
    chan = b_grad.shape[2]
    copies = []

    def store(src, dst):
        copy = pltpu.make_async_copy(src, dst, sem.at[len(copies)])
        copy.start()
        copies.append(copy)

    store(block_in, block_out)
    store(ing_in, in_grad)
    for k, value in enumerate(sums):
        wide[k] = value[...].astype(F32)
        if k < 4:
            store(wide.at[k], glu_grad.at[:, pl.ds(k * chan, chan)])
        elif k < 6:
            for n in range(2):
                store(wide.at[k, pl.ds(n * chan, chan)], c_grad.at[n, :, pl.ds((k - 4) * chan, chan)])
        else:
            store(wide.at[k], b_grad.at[k - 6])
    row = 0
    for ref in (gain, skip, nu, theta, gamma):
        ref[...] = small[row : row + ref.shape[0], :]
        row += ref.shape[0]
    for copy in copies:
        copy.wait()


def on_device(seq, dp, tokens, lengths, gain, b_proj, c_proj, skip, nu, theta, gamma_log, glu, out_grad):
    _, count, width = tokens.shape
    chan = nu.shape[0]
    at = Place(seq, dp)
    blocks = count // STEPS
    anywhere = pl.BlockSpec(memory_space=pl.ANY)
    vmem = pl.BlockSpec(memory_space=pltpu.VMEM)
    dma = pltpu.SemaphoreType.DMA
    wide, low = pltpu.VMEM((count, width), F32), pltpu.VMEM((count, width), BF16)
    specs = unit_specs(at)
    held = pl.pallas_call(
        functools.partial(kernel, at),
        out_shape=(
            pltpu.VMEM(tokens.shape, BF16),
            pltpu.VMEM(tokens.shape, BF16),
            [pltpu.VMEM((ROWS, chan), BF16) for _ in specs],
            pltpu.VMEM((16, LANES), F32),
        ),
        in_specs=[anywhere] * 11,
        out_specs=(vmem, vmem, [vmem] * len(specs), vmem),
        scratch_shapes=[
            low, low,
            pltpu.VMEM((width, 2 * chan), BF16),
            pltpu.VMEM((2 * chan, width), BF16),
            pltpu.VMEM((width, 2 * width), BF16),
            low,
            wide,
            pltpu.VMEM((count, 1), F32),
            low,
            wide, wide,
            low, low,
            *[pltpu.VMEM((width, count), BF16)] * 3,
            pltpu.VMEM((count, 2 * width), BF16),
            low,
            wide,
            pltpu.VMEM((TILE, TILE), BF16),
            pltpu.VMEM((TILE, TILE), BF16),
            pltpu.VMEM((blocks, 2 * chan), F32),
            pltpu.VMEM((blocks, 2 * chan), F32),
            pltpu.VMEM((2, 1, 2 * chan), F32),
            pltpu.VMEM((2, seq, 1, 2 * chan), F32),
            pltpu.VMEM((len(specs), ROWS, chan), BF16),
            [Sum.scratch(at, chan, first, last) for first, last in specs],
            pltpu.VMEM((2, 16, LANES), F32),
            pltpu.VMEM((at.near_count, 16, LANES), F32),
            pltpu.VMEM((at.far_count, 16, LANES), F32),
            pltpu.SMEM(lengths.shape, jnp.int32),
            pltpu.VMEM((1, 3 * chan + 2 * width), F32),
            dma((count // TILE + 6,)),
            dma((2,)),
            dma((2,)),
            dma((3,)),
            dma((3,)),
        ],
        compiler_params=pltpu.CompilerParams(
            collective_id=0, has_side_effects=True, vmem_limit_bytes=40 * 2**20
        ),
    )(
        *(
            pltpu.with_memory_space_constraint(value, pltpu.HBM)
            for value in (
                tokens, out_grad, b_proj, c_proj, glu, lengths,
                gain[None], skip[None], nu[None], theta[None], gamma_log[None],
            )
        )
    )
    lines = [(k, LANES) for k in (width // LANES,) * 2 + (chan // LANES,) * 3]
    block_out, in_grad, b_grad, c_grad, glu_grad, *rest = pl.pallas_call(
        finish,
        out_shape=(
            jax.ShapeDtypeStruct(tokens.shape, BF16),
            jax.ShapeDtypeStruct(tokens.shape, BF16),
            jax.ShapeDtypeStruct(b_proj.shape, F32),
            jax.ShapeDtypeStruct(c_proj.shape, F32),
            jax.ShapeDtypeStruct(glu.shape, F32),
        ) + tuple(jax.ShapeDtypeStruct(line, F32) for line in lines),
        in_specs=[vmem, vmem, [vmem] * len(specs), vmem],
        out_specs=(anywhere,) * 5 + (vmem,) * 5,
        scratch_shapes=[pltpu.VMEM((len(specs), ROWS, chan), F32), dma((12,))],
        compiler_params=pltpu.CompilerParams(vmem_limit_bytes=16 * 2**20),
    )(*held)
    gain_grad, skip_grad, nu_grad, theta_grad, gamma_grad = (value.reshape(-1) for value in rest)
    return (
        block_out, in_grad, gain_grad, b_grad, c_grad, skip_grad, nu_grad, theta_grad, gamma_grad, glu_grad,
    )


def solution(mesh):
    rows, whole = P("dp", "seq", None), P()
    return jax.shard_map(
        functools.partial(on_device, mesh.shape["seq"], mesh.shape["dp"]),
        mesh=mesh,
        in_specs=(rows, P("dp", None)) + (whole,) * 8 + (rows,),
        out_specs=(rows, rows) + (whole,) * 8,
        check_vma=False,
    )
```

time: 56.8 us -> 52.3 us (0.921)
  Pallas kernels: 56 us -> 51.5 us
    pallas_call x1, Pallas kernels: 52.7 us -> 48.2 us  [on_device(): pl.pallas_call(functools.partial(kernel, at), out_shape=(pltpu.VMEM(token...]
where the time goes in v2:
time: 52.3 us; the launch traced here: 52.2 us
  Pallas kernels  51.5 us (98%)
  between operations  0.65 us (1%)
    pallas_call x1, Pallas kernels, on_device(): pl.pallas_call(functools.partial(kernel, at), out_shape=(pltpu.VMEM(token...  48.2 us
    pallas_call x1, Pallas kernels, on_device(): pl.pallas_call(finish, out_shape=(jax.ShapeDtypeStruct(tokens.shape, BF16...  3.36 us

profile of v2, /device:TPU:0, one launch (start us, length us, event | category | flops | bytes accessed | tf_op | source)
XLA Modules:
  0.0 52.2 jit_solution(5628568477247530466)
XLA Ops:
  0.6 48.2 %shard_map.186 = (bf16[1,1024,512]{2,1,0:T(8,128)(2,1)S(1)}, bf16[1,1024,512]{2,1,0:T(8,128)(2,1)S(1)}, bf16[512,256]{1,0:T(8,128)(2,1)S(1)}, bf16[512,256]{1,0:...) custom-call(bf16[1,1024,512]{2,1,0:T(8,128)(2,1)} %tok_hbm.1, ...), custom_call_target="tpu_custom_call" | custom-call | tf_op jit(solution)/shard_map/pallas_call | solution.py:703
  48.8 3.4 %shard_map.187 = (bf16[1,1024,512]{2,1,0:T(8,128)(2,1)}, bf16[1,1024,512]{2,1,0:T(8,128)(2,1)}, f32[2,512,256]{2,1,0:T(8,128)}, f32[2,256,512]{2,1,0:T(8,128)}, ...) custom-call(bf16[1,1024,512]{2,1,0:T(8,128)(2,1)S(1)} %get-tuple-ele, ...), custom_call_target="tpu_custom_call" | custom-call | tf_op jit(solution)/shard_map/pallas_call | solution.py:760

commit v3 on v2

--- a/solution.py
+++ b/solution.py
@@ -11,7 +11,9 @@
 MESH = pl.DeviceIdType.MESH
 F32, BF16 = jnp.float32, jnp.bfloat16
 EPS = 1e-5
+GROUP = 4
 TILE = 256
+CHUNK = 256
 LANES = 128
 SUB = 8
 STEPS = TILE // SUB
@@ -36,6 +38,17 @@
     for _ in range(times):
         a = cmul(a, a)
     return a
+
+
+def chunks(i):
+    for k in range(TILE // CHUNK):
+        yield pl.ds(pl.multiple_of(i * TILE + k * CHUNK, CHUNK), CHUNK), slice(k * CHUNK, (k + 1) * CHUNK)
+
+
+def weave(parts):
+    parts = list(parts)
+    while parts:
+        parts = [part for part in parts if next(part, True) is None]
 
 
 def fold(value):
@@ -280,7 +293,7 @@
     at,
     tok_hbm, og_hbm, b_hbm, c_hbm, glu_hbm, len_hbm, gain_hbm, skip_hbm, nu_hbm, theta_hbm, gam_hbm,
     block_ref, ing_ref, out_refs, small_ref,
-    tok, og, bw, cw, gw, bout, xhat, rstd, u, x, h, hl, dg, ut, ht, gt, dz, dy, dh, order, back_order,
+    tok, og, bw, cw, gw, bout, xhat, rstd, u, x, h, hl, dg, ut, ht, gt, dz, dy, dh, slope, g, order, back_order,
     edge, init, msg, rmsg, part, units, smc, smn, smf,
     len_ref, vectors,
     load_sem, msend, mrecv, ssend, srecv,
@@ -365,22 +378,30 @@
 
     take(bw, load_sem.at[2])
 
-    def front(i, carry):
+    def front_tile(i):
         rows = tile_rows(i)
         tok_in(i).wait()
-        value = mm(order[...], tok[rows, :])
-        tok[rows, :] = value.astype(BF16)
-        centered = value - jnp.mean(value, axis=1, keepdims=True)
-        inv = lax.rsqrt(jnp.mean(centered * centered, axis=1, keepdims=True) + EPS)
-        normal = centered * inv
-        xhat[rows, :] = normal
-        rstd[rows, :] = inv
-        low = (normal * gain).astype(BF16)
-        u[rows, :] = low
-        x[rows, :] = mm(low, bw[...]).astype(BF16).astype(F32) * scale2
+        values = mm(order[...], tok[rows, :])
+        yield
+        for here, part in chunks(i):
+            value = values[part]
+            tok[here, :] = value.astype(BF16)
+            centered = value - jnp.mean(value, axis=1, keepdims=True)
+            inv = lax.rsqrt(jnp.mean(centered * centered, axis=1, keepdims=True) + EPS)
+            normal = centered * inv
+            xhat[here, :] = normal
+            rstd[here, :] = inv
+            u[here, :] = (normal * gain).astype(BF16)
+        drive = mm(u[rows, :], bw[...])
+        yield
+        for here, part in chunks(i):
+            x[here, :] = drive[part].astype(BF16).astype(F32) * scale2
+
+    def front(k, carry):
+        weave(front_tile(k * GROUP + n) for n in range(GROUP))
         return carry
 
-    lax.fori_loop(0, tiles, front, 0)
+    lax.fori_loop(0, tiles // GROUP, front, 0)
 
     def at_step(i, j, count=SUB):
         return pl.ds(pl.multiple_of(i * TILE + j * SUB, count), count)
@@ -468,36 +489,51 @@
     take(gw, load_sem.at[4])
     take(og, load_sem.at[5])
 
-    def middle(i, skip_sum):
+    def middle_tile(i, n, sums_of):
         rows = tile_rows(i)
-        ul = u[rows, :].astype(F32)
-        v = mm(hl[rows, :], cw[...]) + skip * ul
-        square = v * v
-        t = jnp.tanh(v * (0.7978845608028654 + 0.7978845608028654 * 0.044715 * square))
-        half = 0.5 + 0.5 * t
-        wide = v * half
-        slope = half + wide * (1.0 - half) * (2 * 0.7978845608028654 + 6 * 0.7978845608028654 * 0.044715 * square)
-        gl = wide.astype(BF16)
-        gt[:, rows] = gl.T
         ht[:, rows] = hl[rows, :].T
-        value = mm(gl, gw[:, :width])
-        s = 0.5 + 0.5 * jnp.tanh(0.5 * mm(gl, gw[:, width:]))
-        branch = value * s
-        bout[rows, :] = (tok[rows, :].astype(F32) + branch).astype(BF16)
-        cot = mm(order[...], og[rows, :])
-        og[rows, :] = cot.astype(BF16)
-        scaled = cot * s
-        dvalue = scaled.astype(BF16)
-        dgate = (scaled * (value - branch)).astype(BF16)
-        dz[rows, :width] = dvalue
-        dz[rows, width:] = dgate
-        back = mm(dvalue, gw[:, :width], NT) + mm(dgate, gw[:, width:], NT)
-        dyl = (back * slope).astype(BF16)
-        dy[rows, :] = dyl
-        dh[rows, :] = mm(dyl, cw[...], NT).astype(BF16).astype(F32)
-        return skip_sum + fold(dyl.astype(F32) * ul)
-
-    skip_sum = lax.fori_loop(0, tiles, middle, jnp.zeros((8, width), F32))
+        mixed = mm(hl[rows, :], cw[...])
+        yield
+        for here, part in chunks(i):
+            v = mixed[part] + skip * u[here, :].astype(F32)
+            square = v * v
+            t = jnp.tanh(v * (0.7978845608028654 + 0.7978845608028654 * 0.044715 * square))
+            half = 0.5 + 0.5 * t
+            wide = v * half
+            slope[n, part, :] = half + wide * (1.0 - half) * (
+                2 * 0.7978845608028654 + 6 * 0.7978845608028654 * 0.044715 * square
+            )
+            g[n, part, :] = wide.astype(BF16)
+        gt[:, rows] = g[n].T
+        values, gates = mm(g[n], gw[:, :width]), mm(g[n], gw[:, width:])
+        cots = mm(order[...], og[rows, :])
+        yield
+        for here, part in chunks(i):
+            value, cot = values[part], cots[part]
+            s = 0.5 + 0.5 * jnp.tanh(0.5 * gates[part])
+            branch = value * s
+            bout[here, :] = (tok[here, :].astype(F32) + branch).astype(BF16)
+            og[here, :] = cot.astype(BF16)
+            scaled = cot * s
+            dz[here, :width] = scaled.astype(BF16)
+            dz[here, width:] = (scaled * (value - branch)).astype(BF16)
+        back = mm(dz[rows, :], gw[...], NT)
+        yield
+        for here, part in chunks(i):
+            dyl = (back[part] * slope[n, part, :]).astype(BF16)
+            dy[here, :] = dyl
+            sums_of.append(fold(dyl.astype(F32) * u[here, :].astype(F32)))
+        cot_h = mm(dy[rows, :], cw[...], NT)
+        yield
+        for here, part in chunks(i):
+            dh[here, :] = cot_h[part].astype(BF16).astype(F32)
+
+    def middle(k, skip_sum):
+        sums_of = [skip_sum]
+        weave(middle_tile(k * GROUP + n, n, sums_of) for n in range(GROUP))
+        return functools.reduce(jnp.add, sums_of)
+
+    skip_sum = lax.fori_loop(0, tiles // GROUP, middle, jnp.zeros((8, width), F32))
 
     def retreat(k, carry):
         j = STEPS - 1 - k
@@ -518,18 +554,25 @@
     def multiply(pair):
         left, right, column = factors[pair]
         half = ROWS // 2
-        for core in (1 - at.c, at.c):
+        here = pl.ds(column * chan, 2 * chan)
+
+        def one_half(k, carry):
+            core = jnp.where(k == 0, 1 - at.c, at.c)
             rows = pl.ds(pl.multiple_of(core * half, half), half)
-
-            def columns(n, carry, rows=rows):
-                here = pl.ds(pl.multiple_of((column + n) * chan, chan), chan)
-                part[2 * pair + n, rows, :] = mm(left[rows, :], right[:, here]).astype(BF16)
-                return carry
-
-            lax.fori_loop(0, 2, columns, 0)
-            if core is not at.c:
+            product = mm(left[rows, :], right[:, here]).astype(BF16)
+            part[2 * pair, rows, :] = product[:, :chan]
+            part[2 * pair + 1, rows, :] = product[:, chan:]
+
+            @pl.when(k == 0)
+            def _():
                 for n in range(2):
                     sums[2 * pair + n].start_core()
+
+            return carry
+
+        lax.fori_loop(0, 2, one_half, 0)
+        for n in range(2):
+            sums[2 * pair + n].sent = half
 
     def run(point):
         for step in PLAN[point]:
@@ -625,20 +668,31 @@
     lax.fori_loop(0, tiles, put_block, 0)
     run(4)
 
-    def last_tile(i, gain_sum):
+    def last_tile(i, sums_of):
         rows = tile_rows(i)
-        du = mm(dg[rows, :], bw[...], NT) + skip * dy[rows, :].astype(F32)
-        normal = xhat[rows, :]
-        e = gain * du
-        mean_e = jnp.mean(e, axis=1, keepdims=True)
-        mean_ex = jnp.mean(e * normal, axis=1, keepdims=True)
-        grad = og[rows, :].astype(F32) + (e - mean_e - normal * mean_ex) * rstd[rows, :]
-        ing_ref[0, rows, :] = mm(back_order[...], grad.astype(BF16)).astype(BF16)
-        return gain_sum + fold(du * normal)
-
-    gain_sum = lax.fori_loop(0, tiles // 2, last_tile, jnp.zeros((8, width), F32))
+        dus = mm(dg[rows, :], bw[...], NT)
+        yield
+        for here, part in chunks(i):
+            du = dus[part] + skip * dy[here, :].astype(F32)
+            normal = xhat[here, :]
+            e = gain * du
+            mean_e = jnp.mean(e, axis=1, keepdims=True)
+            mean_ex = jnp.mean(e * normal, axis=1, keepdims=True)
+            grad = og[here, :].astype(F32) + (e - mean_e - normal * mean_ex) * rstd[here, :]
+            og[here, :] = grad.astype(BF16)
+            sums_of.append(fold(du * normal))
+        result = mm(back_order[...], og[rows, :])
+        yield
+        ing_ref[0, rows, :] = result.astype(BF16)
+
+    def last(k, gain_sum):
+        sums_of = [gain_sum]
+        weave(last_tile(k * 2 + n, sums_of) for n in range(2))
+        return functools.reduce(jnp.add, sums_of)
+
+    gain_sum = last(0, jnp.zeros((8, width), F32))
     run(5)
-    gain_sum = lax.fori_loop(tiles // 2, tiles, last_tile, gain_sum)
+    gain_sum = lax.fori_loop(1, tiles // 2, last, gain_sum)
 
     small = [
         jnp.sum(gain_sum, axis=0, keepdims=True),
@@ -725,6 +779,8 @@
             pltpu.VMEM((count, 2 * width), BF16),
             low,
             wide,
+            pltpu.VMEM((GROUP, TILE, width), F32),
+            pltpu.VMEM((GROUP, TILE, width), BF16),
             pltpu.VMEM((TILE, TILE), BF16),
             pltpu.VMEM((TILE, TILE), BF16),
             pltpu.VMEM((blocks, 2 * chan), F32),

time: 52.3 us -> 49.7 us (0.950)
  Pallas kernels: 51.5 us -> 48.9 us
    pallas_call x1, Pallas kernels: 48.2 us -> 45.6 us  [on_device(): pl.pallas_call(functools.partial(kernel, at), out_shape=(pltpu.VMEM(token...]
where the time goes in v3:
time: 49.7 us; the launch traced here: 49.6 us
  Pallas kernels  48.9 us (98%)
  between operations  0.65 us (1%)
    pallas_call x1, Pallas kernels, on_device(): pl.pallas_call(functools.partial(kernel, at), out_shape=(pltpu.VMEM(token...  45.6 us
    pallas_call x1, Pallas kernels, on_device(): pl.pallas_call(finish, out_shape=(jax.ShapeDtypeStruct(tokens.shape, BF16...  3.36 us

profile of v3, /device:TPU:0, one launch (start us, length us, event | category | flops | bytes accessed | tf_op | source)
XLA Modules:
  0.0 49.6 jit_solution(10078759258703456913)
XLA Ops:
  0.6 45.6 %shard_map.186 = (bf16[1,1024,512]{2,1,0:T(8,128)(2,1)S(1)}, bf16[1,1024,512]{2,1,0:T(8,128)(2,1)S(1)}, bf16[512,256]{1,0:T(8,128)(2,1)S(1)}, bf16[512,256]{1,0:...) custom-call(bf16[1,1024,512]{2,1,0:T(8,128)(2,1)} %tok_hbm.1, ...), custom_call_target="tpu_custom_call" | custom-call | tf_op jit(solution)/shard_map/pallas_call | solution.py:757
  46.2 3.4 %shard_map.187 = (bf16[1,1024,512]{2,1,0:T(8,128)(2,1)}, bf16[1,1024,512]{2,1,0:T(8,128)(2,1)}, f32[2,512,256]{2,1,0:T(8,128)}, f32[2,256,512]{2,1,0:T(8,128)}, ...) custom-call(bf16[1,1024,512]{2,1,0:T(8,128)(2,1)S(1)} %get-tuple-ele, ...), custom_call_target="tpu_custom_call" | custom-call | tf_op jit(solution)/shard_map/pallas_call | solution.py:816

commit v4 on v3

--- a/solution.py
+++ b/solution.py
@@ -11,6 +11,7 @@
 MESH = pl.DeviceIdType.MESH
 F32, BF16 = jnp.float32, jnp.bfloat16
 EPS = 1e-5
+MIDDLE = 512
 GROUP = 4
 TILE = 256
 CHUNK = 256
@@ -18,12 +19,10 @@
 SUB = 8
 STEPS = TILE // SUB
 ROWS = 512
-NT = (((1,), (1,)), ((), ()))
-TN = (((0,), (0,)), ((), ()))
-
-
-def mm(a, b, dims=(((1,), (0,)), ((), ()))):
-    return lax.dot_general(a, b, dims, preferred_element_type=F32)
+
+
+def mm(a, b):
+    return jnp.dot(a, b, preferred_element_type=F32)
 
 
 def add(a, b):
@@ -40,9 +39,9 @@
     return a
 
 
-def chunks(i):
-    for k in range(TILE // CHUNK):
-        yield pl.ds(pl.multiple_of(i * TILE + k * CHUNK, CHUNK), CHUNK), slice(k * CHUNK, (k + 1) * CHUNK)
+def chunks(i, tile=TILE):
+    for k in range(tile // CHUNK):
+        yield pl.ds(pl.multiple_of(i * tile + k * CHUNK, CHUNK), CHUNK), slice(k * CHUNK, (k + 1) * CHUNK)
 
 
 def weave(parts):
@@ -267,22 +266,13 @@
 
 
 PLAN = (
-    ("m01", "m23", "m45", "a0", "a1", "a2", "a3", "n3",),
     (),
-    ("a4", "a5", "n5",),
-    ("m67",),
+    ("m01", "m23", "m45", "a0", "n0", "a1", "a2", "a3", "n3", ),
     (),
-    ("a6", "a7", "n0", "n1", "n2",),
-    (
-        "s0", "n4", "f3", "s1", "f5", "n6", "n7", "f0", "f1", "f2", "b3", "f4", "s2", "b5",
-        "f6", "f7", "b0", "b1", "b2", "s3", "x3", "b4", "x5", "b6", "c3", "e3", "b7", "x0",
-        "x1", "x2", "x4", "c0", "e0", "c5", "e5", "x6", "c1", "x7", "c2", "c6", "e6", "c4",
-        "e1", "c7", "e7", "e2", "e4",
-    ),
+    ("a4", "n4", "a5", ),
+    ("m67", "p0", "l0", "a6", "a7", "n7", "f0", "n1", "n2", "l1", "s0", "f3", "s1", "n5", "f4", "n6", "b0", "f1", "f7", "f2", "b3", "s2", "f5", "b4", "f6", "x0", "b1", "b7", "x3", "b2", "s3", "b5", "x4", "b6", "c0", "x1", "c4", "e4", "x7", "e0", "x2", "c3", "e3", "x5", "c1", "x6", "c7", "c5", "e5", "c2", "e1", "c6", "e6", "e7", "e2", ),
 )
-AXES = (
-    (0, None), (1, 1), (2, 2), (None, None), (0, 0), (None, 0), (1, None), (0, None),
-)
+AXES = ((None, 1), (1, 1), (0, 0), (None, 0), (None, None), (2, None), (1, None), (None, 2))
 
 
 def unit_specs(at):
@@ -293,7 +283,7 @@
     at,
     tok_hbm, og_hbm, b_hbm, c_hbm, glu_hbm, len_hbm, gain_hbm, skip_hbm, nu_hbm, theta_hbm, gam_hbm,
     block_ref, ing_ref, out_refs, small_ref,
-    tok, og, bw, cw, gw, bout, xhat, rstd, u, x, h, hl, dg, ut, ht, gt, dz, dy, dh, slope, g, order, back_order,
+    tok, og, bw, cw, gw, bout, xhat, rstd, u, x, h, hl, dg, bt, ct, gwt, ut, ht, gt, dz, dy, dh, slope, g, order, back_order,
     edge, init, msg, rmsg, part, units, smc, smn, smf,
     len_ref, vectors,
     load_sem, msend, mrecv, ssend, srecv,
@@ -332,10 +322,6 @@
         load(b_hbm.at[k], bw.at[:, pl.ds(k * chan, chan)], 2)
     for i in range(1, tiles):
         tok_in(i).start()
-    for k in range(2):
-        load(c_hbm.at[k], cw.at[pl.ds(k * chan, chan)], 3)
-    load(glu_hbm, gw, 4)
-    load(og_hbm.at[0], og, 5)
 
     first = lax.broadcasted_iota(jnp.int32, (TILE, TILE), 0)
     second = lax.broadcasted_iota(jnp.int32, (TILE, TILE), 1)
@@ -402,6 +388,10 @@
         return carry
 
     lax.fori_loop(0, tiles // GROUP, front, 0)
+    for k in range(2):
+        load(c_hbm.at[k], cw.at[pl.ds(k * chan, chan)], 3)
+    load(glu_hbm, gw, 4)
+    load(og_hbm.at[0], og, 5)
 
     def at_step(i, j, count=SUB):
         return pl.ds(pl.multiple_of(i * TILE + j * SUB, count), count)
@@ -435,20 +425,30 @@
     for k in range(blocks):
         state = add(edge_row(k), cmul(conj_step, kept(k, state)))
 
-    others = pl.ds(1, seq - 1)
+    def pairs(ahead):
+        for o in range(seq - 1, 0, -1):
+            to = at.s - o if ahead else at.s + o
+            source = at.s + o if ahead else at.s - o
+            yield o, (to >= 0 if ahead else to < seq), (to, at.d), (source < seq if ahead else source >= 0)
+
+    def edge_copy(which, o, device):
+        return pltpu.make_async_remote_copy(
+            src_ref=msg.at[which], dst_ref=rmsg.at[which, o], send_sem=msend.at[which, o],
+            recv_sem=mrecv.at[which, o], device_id=device, device_id_type=MESH,
+        )
 
     def exchange(which, value):
         msg[which] = both(value)
-        for o in range(seq - 1, 0, -1):
-            remote(msg.at[which], rmsg.at[which, o], msend.at[which], mrecv.at[which], at.group(o))
+        for o, needed, device, _ in pairs(which == 1):
+            pl.when(needed)(edge_copy(which, o, device).start)
 
     def gather(which, factor, ahead):
-        take(rmsg.at[which, others], mrecv.at[which])
+        for o, _, device, coming in pairs(ahead):
+            pl.when(coming)(edge_copy(which, o, device).wait_recv)
         result = zero_row
         for o in range(seq - 1, 0, -1):
             source = at.s + o if ahead else at.s - o
-            slot = seq - o if ahead else o
-            there = (rmsg[which, slot, :, lo], rmsg[which, slot, :, hi])
+            there = (rmsg[which, o, :, lo], rmsg[which, o, :, hi])
             k = keep_all(source)
             new = add(there, cmul((factor[0] * k, factor[1] * k), result))
             valid = source < seq if ahead else source >= 0
@@ -463,6 +463,19 @@
         return carry
 
     lax.fori_loop(0, tiles, turn_u, 0)
+    for k in range(2):
+        bt[k * chan : (k + 1) * chan, :] = bw[:, k * chan : (k + 1) * chan].T
+    take(cw, load_sem.at[3])
+    for k in range(2):
+        ct[:, k * chan : (k + 1) * chan] = cw[k * chan : (k + 1) * chan, :].T
+    take(gw, load_sem.at[4])
+
+    def turn_glu(k, carry):
+        here = pl.ds(pl.multiple_of(k * chan, chan), chan)
+        gwt[here, :] = gw[:, here].T
+        return carry
+
+    lax.fori_loop(0, gw.shape[1] // chan, turn_glu, 0)
     carry = gather(0, conj_all, False)
 
     for k in range(blocks):
@@ -485,16 +498,14 @@
 
     lax.fori_loop(0, STEPS // 2, advance_store, [pick_tile(init, i) for i in range(tiles)], unroll=2)
 
-    take(cw, load_sem.at[3])
-    take(gw, load_sem.at[4])
     take(og, load_sem.at[5])
 
     def middle_tile(i, n, sums_of):
-        rows = tile_rows(i)
+        rows = pl.ds(pl.multiple_of(i * MIDDLE, MIDDLE), MIDDLE)
         ht[:, rows] = hl[rows, :].T
         mixed = mm(hl[rows, :], cw[...])
         yield
-        for here, part in chunks(i):
+        for here, part in chunks(i, MIDDLE):
             v = mixed[part] + skip * u[here, :].astype(F32)
             square = v * v
             t = jnp.tanh(v * (0.7978845608028654 + 0.7978845608028654 * 0.044715 * square))
@@ -506,10 +517,12 @@
             g[n, part, :] = wide.astype(BF16)
         gt[:, rows] = g[n].T
         values, gates = mm(g[n], gw[:, :width]), mm(g[n], gw[:, width:])
-        cots = mm(order[...], og[rows, :])
+        cots = [
+            mm(order[...], og[tile_rows(i * (MIDDLE // TILE) + k), :]) for k in range(MIDDLE // TILE)
+        ]
         yield
-        for here, part in chunks(i):
-            value, cot = values[part], cots[part]
+        for here, part in chunks(i, MIDDLE):
+            value, cot = values[part], cots[part.start // TILE]
             s = 0.5 + 0.5 * jnp.tanh(0.5 * gates[part])
             branch = value * s
             bout[here, :] = (tok[here, :].astype(F32) + branch).astype(BF16)
@@ -517,33 +530,24 @@
             scaled = cot * s
             dz[here, :width] = scaled.astype(BF16)
             dz[here, width:] = (scaled * (value - branch)).astype(BF16)
-        back = mm(dz[rows, :], gw[...], NT)
+        back = mm(dz[rows, :], gwt[...])
         yield
-        for here, part in chunks(i):
+        for here, part in chunks(i, MIDDLE):
             dyl = (back[part] * slope[n, part, :]).astype(BF16)
             dy[here, :] = dyl
             sums_of.append(fold(dyl.astype(F32) * u[here, :].astype(F32)))
-        cot_h = mm(dy[rows, :], cw[...], NT)
+        cot_h = mm(dy[rows, :], ct[...])
         yield
-        for here, part in chunks(i):
+        for here, part in chunks(i, MIDDLE):
             dh[here, :] = cot_h[part].astype(BF16).astype(F32)
 
     def middle(k, skip_sum):
         sums_of = [skip_sum]
-        weave(middle_tile(k * GROUP + n, n, sums_of) for n in range(GROUP))
+        count = tokens // MIDDLE
+        weave(middle_tile(k * count + n, n, sums_of) for n in range(count))
         return functools.reduce(jnp.add, sums_of)
 
-    skip_sum = lax.fori_loop(0, tiles // GROUP, middle, jnp.zeros((8, width), F32))
-
-    def retreat(k, carry):
-        j = STEPS - 1 - k
-        return [cmul(lam, add(pick(dh, i, j), carry[i])) for i in range(tiles)]
-
-    keep_edges(lax.fori_loop(0, STEPS, retreat, [nothing] * tiles, unroll=4))
-    state = zero_row
-    for k in range(blocks - 1, -1, -1):
-        state = kept(k, add(edge_row(k), cmul(lam_step, state)))
-    exchange(1, state)
+    skip_sum = middle(0, jnp.zeros((8, width), F32))
 
     sums = [
         Sum(at, first, last, out, part.at[k], *refs)
@@ -573,6 +577,50 @@
         lax.fori_loop(0, 2, one_half, 0)
         for n in range(2):
             sums[2 * pair + n].sent = half
+
+    def put_block(i, carry):
+        block_ref[0, tile_rows(i), :] = mm(back_order[...], bout[tile_rows(i), :]).astype(BF16)
+        return carry
+
+    def last_tile(i, sums_of):
+        rows = tile_rows(i)
+        dus = mm(dg[rows, :], bt[...])
+        yield
+        for here, part in chunks(i):
+            du = dus[part] + skip * dy[here, :].astype(F32)
+            normal = xhat[here, :]
+            e = gain * du
+            mean_e = jnp.mean(e, axis=1, keepdims=True)
+            mean_ex = jnp.mean(e * normal, axis=1, keepdims=True)
+            grad = og[here, :].astype(F32) + (e - mean_e - normal * mean_ex) * rstd[here, :]
+            og[here, :] = grad.astype(BF16)
+            sums_of.append(fold(du * normal))
+        result = mm(back_order[...], og[rows, :])
+        yield
+        ing_ref[0, rows, :] = result.astype(BF16)
+
+    def last(k, gain_sum):
+        sums_of = [gain_sum]
+        weave(last_tile(k * 2 + n, sums_of) for n in range(2))
+        return functools.reduce(jnp.add, sums_of)
+
+    found = {}
+
+    def fill_small():
+        small = [
+            jnp.sum(found["gain"], axis=0, keepdims=True),
+            jnp.sum(skip_sum, axis=0, keepdims=True),
+            -jnp.exp(nu) * (lam[0] * found["sums"][0] + lam[1] * found["sums"][1]),
+            angle * (lam[0] * found["sums"][1] - lam[1] * found["sums"][0]),
+            found["sums"][2],
+        ]
+        row = 0
+        for value in small:
+            for k in range(value.shape[1] // LANES):
+                smc[at.c, row : row + 1, :] = value[:, k * LANES : (k + 1) * LANES]
+                row += 1
+        smc[at.c, row:, :] = jnp.zeros((smc.shape[1] - row, LANES), F32)
+
 
     def run(point):
         for step in PLAN[point]:
@@ -582,6 +630,10 @@
             for k in map(int, step[1:]):
                 if step[0] == "s":
                     small_stage(k)
+                elif step[0] == "p":
+                    lax.fori_loop(0, tiles, put_block, 0)
+                elif step[0] == "l":
+                    found["gain"] = last(k, found.get("gain", jnp.zeros((8, width), F32)))
                 else:
                     getattr(sums[k], STAGES[step[0]])()
 
@@ -601,6 +653,7 @@
 
     def small_stage(k):
         if k == 0:
+            fill_small()
             spread(0, smc, at.c, [at.core()])
         elif k == 1:
             smn[at.q] = collect(0, smc)
@@ -613,8 +666,20 @@
 
     run(0)
 
+    def retreat(k, carry):
+        j = STEPS - 1 - k
+        return [cmul(lam, add(pick(dh, i, j), carry[i])) for i in range(tiles)]
+
+    keep_edges(lax.fori_loop(0, STEPS, retreat, [nothing] * tiles, unroll=4))
+    state = zero_row
+    for k in range(blocks - 1, -1, -1):
+        state = kept(k, add(edge_row(k), cmul(lam_step, state)))
+    exchange(1, state)
+
+    run(1)
+
     incoming = gather(1, lam_all, True)
-    run(1)
+    run(2)
     for k in range(blocks - 1, -1, -1):
         if k > 0:
             following = kept(k, add(edge_row(k), cmul(lam_step, incoming)))
@@ -656,61 +721,13 @@
     carry, late = adjoint(1, carry, before_of(1))
     carry, early = adjoint(0, carry, [pick_tile(init, i) for i in range(tiles)])
     put_pair(0, early, late)
-    pre, pim, gsum = (jnp.sum(value, axis=0, keepdims=True) for value in carry[1])
-
-    run(2)
+    found["sums"] = [jnp.sum(value, axis=0, keepdims=True) for value in carry[1]]
+
     run(3)
-
-    def put_block(i, carry):
-        block_ref[0, tile_rows(i), :] = mm(back_order[...], bout[tile_rows(i), :]).astype(BF16)
-        return carry
-
-    lax.fori_loop(0, tiles, put_block, 0)
     run(4)
-
-    def last_tile(i, sums_of):
-        rows = tile_rows(i)
-        dus = mm(dg[rows, :], bw[...], NT)
-        yield
-        for here, part in chunks(i):
-            du = dus[part] + skip * dy[here, :].astype(F32)
-            normal = xhat[here, :]
-            e = gain * du
-            mean_e = jnp.mean(e, axis=1, keepdims=True)
-            mean_ex = jnp.mean(e * normal, axis=1, keepdims=True)
-            grad = og[here, :].astype(F32) + (e - mean_e - normal * mean_ex) * rstd[here, :]
-            og[here, :] = grad.astype(BF16)
-            sums_of.append(fold(du * normal))
-        result = mm(back_order[...], og[rows, :])
-        yield
-        ing_ref[0, rows, :] = result.astype(BF16)
-
-    def last(k, gain_sum):
-        sums_of = [gain_sum]
-        weave(last_tile(k * 2 + n, sums_of) for n in range(2))
-        return functools.reduce(jnp.add, sums_of)
-
-    gain_sum = last(0, jnp.zeros((8, width), F32))
-    run(5)
-    gain_sum = lax.fori_loop(1, tiles // 2, last, gain_sum)
-
-    small = [
-        jnp.sum(gain_sum, axis=0, keepdims=True),
-        jnp.sum(skip_sum, axis=0, keepdims=True),
-        -jnp.exp(nu) * (lam[0] * pre + lam[1] * pim),
-        angle * (lam[0] * pim - lam[1] * pre),
-        gsum,
-    ]
-    row = 0
-    for value in small:
-        for k in range(value.shape[1] // LANES):
-            smc[at.c, row : row + 1, :] = value[:, k * LANES : (k + 1) * LANES]
-            row += 1
-    smc[at.c, row:, :] = jnp.zeros((smc.shape[1] - row, LANES), F32)
-
-    run(6)
     for which in range(2):
-        take(rmsg.at[which, others], msend.at[which])
+        for o, needed, device, _ in pairs(which == 1):
+            pl.when(needed)(edge_copy(which, o, device).wait_send)
 
 
 def finish(
@@ -775,12 +792,15 @@
             low,
             wide, wide,
             low, low,
+            pltpu.VMEM((2 * chan, width), BF16),
+            pltpu.VMEM((width, 2 * chan), BF16),
+            pltpu.VMEM((2 * width, width), BF16),
             *[pltpu.VMEM((width, count), BF16)] * 3,
             pltpu.VMEM((count, 2 * width), BF16),
             low,
             wide,
-            pltpu.VMEM((GROUP, TILE, width), F32),
-            pltpu.VMEM((GROUP, TILE, width), BF16),
+            pltpu.VMEM((count // MIDDLE, MIDDLE, width), F32),
+            pltpu.VMEM((count // MIDDLE, MIDDLE, width), BF16),
             pltpu.VMEM((TILE, TILE), BF16),
             pltpu.VMEM((TILE, TILE), BF16),
             pltpu.VMEM((blocks, 2 * chan), F32),
@@ -795,13 +815,13 @@
             pltpu.SMEM(lengths.shape, jnp.int32),
             pltpu.VMEM((1, 3 * chan + 2 * width), F32),
             dma((count // TILE + 6,)),
-            dma((2,)),
-            dma((2,)),
+            dma((2, seq)),
+            dma((2, seq)),
             dma((3,)),
             dma((3,)),
         ],
         compiler_params=pltpu.CompilerParams(
-            collective_id=0, has_side_effects=True, vmem_limit_bytes=40 * 2**20
+            collective_id=0, has_side_effects=True, vmem_limit_bytes=48 * 2**20
         ),
     )(
         *(

time: 49.7 us -> 48.4 us (0.974)
  Pallas kernels: 48.9 us -> 47.6 us
    pallas_call x1, Pallas kernels: 45.6 us -> 44.2 us  [on_device(): pl.pallas_call(functools.partial(kernel, at), out_shape=(pltpu.VMEM(token...]
where the time goes in v4:
time: 48.4 us; the launch traced here: 48.2 us
  Pallas kernels  47.6 us (98%)
  between operations  0.65 us (1%)
    pallas_call x1, Pallas kernels, on_device(): pl.pallas_call(functools.partial(kernel, at), out_shape=(pltpu.VMEM(token...  44.2 us
    pallas_call x1, Pallas kernels, on_device(): pl.pallas_call(finish, out_shape=(jax.ShapeDtypeStruct(tokens.shape, BF16...  3.36 us

profile of v4, /device:TPU:0, one launch (start us, length us, event | category | flops | bytes accessed | tf_op | source)
XLA Modules:
  0.0 48.2 jit_solution(9475837822991541941)
XLA Ops:
  0.6 44.2 %shard_map.186 = (bf16[1,1024,512]{2,1,0:T(8,128)(2,1)S(1)}, bf16[1,1024,512]{2,1,0:T(8,128)(2,1)S(1)}, bf16[512,256]{1,0:T(8,128)(2,1)S(1)}, bf16[512,256]{1,0:...) custom-call(bf16[1,1024,512]{2,1,0:T(8,128)(2,1)} %tok_hbm.1, ...), custom_call_target="tpu_custom_call" | custom-call | tf_op jit(solution)/shard_map/pallas_call | solution.py:774
  44.9 3.4 %shard_map.187 = (bf16[1,1024,512]{2,1,0:T(8,128)(2,1)}, bf16[1,1024,512]{2,1,0:T(8,128)(2,1)}, f32[2,512,256]{2,1,0:T(8,128)}, f32[2,256,512]{2,1,0:T(8,128)}, ...) custom-call(bf16[1,1024,512]{2,1,0:T(8,128)(2,1)S(1)} %get-tuple-ele, ...), custom_call_target="tpu_custom_call" | custom-call | tf_op jit(solution)/shard_map/pallas_call | solution.py:836

commit v5 on v4

--- a/solution.py
+++ b/solution.py
@@ -272,7 +272,7 @@
     ("a4", "n4", "a5", ),
     ("m67", "p0", "l0", "a6", "a7", "n7", "f0", "n1", "n2", "l1", "s0", "f3", "s1", "n5", "f4", "n6", "b0", "f1", "f7", "f2", "b3", "s2", "f5", "b4", "f6", "x0", "b1", "b7", "x3", "b2", "s3", "b5", "x4", "b6", "c0", "x1", "c4", "e4", "x7", "e0", "x2", "c3", "e3", "x5", "c1", "x6", "c7", "c5", "e5", "c2", "e1", "c6", "e6", "e7", "e2", ),
 )
-AXES = ((None, 1), (1, 1), (0, 0), (None, 0), (None, None), (2, None), (1, None), (None, 2))
+AXES = ((None, 1), (1, 1), (2, 2), (None, 2), (None, None), (0, None), (1, None), (None, 0))
 
 
 def unit_specs(at):
@@ -284,7 +284,7 @@
     tok_hbm, og_hbm, b_hbm, c_hbm, glu_hbm, len_hbm, gain_hbm, skip_hbm, nu_hbm, theta_hbm, gam_hbm,
     block_ref, ing_ref, out_refs, small_ref,
     tok, og, bw, cw, gw, bout, xhat, rstd, u, x, h, hl, dg, bt, ct, gwt, ut, ht, gt, dz, dy, dh, slope, g, order, back_order,
-    edge, init, msg, rmsg, part, units, smc, smn, smf,
+    edge, init, ends, reach, msg, rmsg, part, units, smc, smn, smf,
     len_ref, vectors,
     load_sem, msend, mrecv, ssend, srecv,
 ):
@@ -421,9 +421,28 @@
     def edge_row(k):
         return edge[k : k + 1, lo], edge[k : k + 1, hi]
 
+    def spread_keeps(factor, ahead):
+        value = (jnp.ones((1, chan), F32), jnp.zeros((1, chan), F32))
+        if ahead:
+            for k in range(blocks - 1, -1, -1):
+                reach[k : k + 1, :] = both(value)
+                value = kept(k, cmul(factor, value))
+        else:
+            for k in range(blocks):
+                value = kept(k, value)
+                reach[k : k + 1, :] = both(value)
+                value = cmul(factor, value)
+
+    def with_carry(ref, carry):
+        change = cmul((reach[:, lo], reach[:, hi]), carry)
+        ref[:, lo] = ref[:, lo] + change[0]
+        ref[:, hi] = ref[:, hi] + change[1]
+
     state = zero_row
     for k in range(blocks):
-        state = add(edge_row(k), cmul(conj_step, kept(k, state)))
+        state = kept(k, state)
+        init[k : k + 1, :] = both(state)
+        state = add(edge_row(k), cmul(conj_step, state))
 
     def pairs(ahead):
         for o in range(seq - 1, 0, -1):
@@ -442,17 +461,21 @@
         for o, needed, device, _ in pairs(which == 1):
             pl.when(needed)(edge_copy(which, o, device).start)
 
-    def gather(which, factor, ahead):
-        for o, _, device, coming in pairs(ahead):
+    def chain(factor, ahead):
+        value, result = (jnp.ones((1, chan), F32), jnp.zeros((1, chan), F32)), {}
+        for o in range(1, seq):
+            result[o] = value
+            k = keep_all(at.s + o if ahead else at.s - o)
+            value = cmul((factor[0] * k, factor[1] * k), value)
+        return result
+
+    def gather(which, way):
+        for o, _, device, coming in pairs(which == 1):
             pl.when(coming)(edge_copy(which, o, device).wait_recv)
         result = zero_row
-        for o in range(seq - 1, 0, -1):
-            source = at.s + o if ahead else at.s - o
-            there = (rmsg[which, o, :, lo], rmsg[which, o, :, hi])
-            k = keep_all(source)
-            new = add(there, cmul((factor[0] * k, factor[1] * k), result))
-            valid = source < seq if ahead else source >= 0
-            result = tuple(jnp.where(valid, a, b) for a, b in zip(new, result))
+        for o, _, _, coming in pairs(which == 1):
+            there = cmul(way[o], (rmsg[which, o, :, lo], rmsg[which, o, :, hi]))
+            result = add(result, tuple(jnp.where(coming, value, 0.0) for value in there))
         return result
 
     pl.semaphore_wait(barrier, len(peers))
@@ -476,13 +499,11 @@
         return carry
 
     lax.fori_loop(0, gw.shape[1] // chan, turn_glu, 0)
-    carry = gather(0, conj_all, False)
-
-    for k in range(blocks):
-        begin = kept(k, carry)
-        init[k : k + 1, :] = both(begin)
-        if k + 1 < blocks:
-            carry = add(edge_row(k), cmul(conj_step, begin))
+    spread_keeps(conj_step, False)
+    way = chain(conj_all, False)
+    carry = gather(0, way)
+
+    with_carry(init, carry)
 
     def advance_store(pair, carry):
         states = [[], []]
@@ -673,20 +694,16 @@
     keep_edges(lax.fori_loop(0, STEPS, retreat, [nothing] * tiles, unroll=4))
     state = zero_row
     for k in range(blocks - 1, -1, -1):
+        ends[k : k + 1, :] = both(state)
         state = kept(k, add(edge_row(k), cmul(lam_step, state)))
     exchange(1, state)
+    spread_keeps(lam_step, True)
+    way = chain(lam_all, True)
 
     run(1)
 
-    incoming = gather(1, lam_all, True)
+    with_carry(ends, gather(1, way))
     run(2)
-    for k in range(blocks - 1, -1, -1):
-        if k > 0:
-            following = kept(k, add(edge_row(k), cmul(lam_step, incoming)))
-        edge[k : k + 1, :] = both(incoming)
-        if k > 0:
-            incoming = following
-
     def adjoint(j, carry, before):
         states, sums_of = carry
         pre, pim, gsum = sums_of
@@ -716,7 +733,7 @@
         put_pair(pair, early, late)
         return carry
 
-    carry = ([pick_tile(edge, i) for i in range(tiles)], (jnp.zeros((SUB, chan), F32),) * 3)
+    carry = ([pick_tile(ends, i) for i in range(tiles)], (jnp.zeros((SUB, chan), F32),) * 3)
     carry = lax.fori_loop(0, STEPS // 2 - 1, adjoint_pair, carry)
     carry, late = adjoint(1, carry, before_of(1))
     carry, early = adjoint(0, carry, [pick_tile(init, i) for i in range(tiles)])
@@ -803,8 +820,7 @@
             pltpu.VMEM((count // MIDDLE, MIDDLE, width), BF16),
             pltpu.VMEM((TILE, TILE), BF16),
             pltpu.VMEM((TILE, TILE), BF16),
-            pltpu.VMEM((blocks, 2 * chan), F32),
-            pltpu.VMEM((blocks, 2 * chan), F32),
+            *[pltpu.VMEM((blocks, 2 * chan), F32)] * 4,
             pltpu.VMEM((2, 1, 2 * chan), F32),
             pltpu.VMEM((2, seq, 1, 2 * chan), F32),
             pltpu.VMEM((len(specs), ROWS, chan), BF16),

time: 48.4 us -> 48 us (level)
  Pallas kernels: 47.6 us -> 47.1 us
where the time goes in v5:
time: 48 us; the launch traced here: 47.8 us
  Pallas kernels  47.1 us (98%)
  between operations  0.65 us (1%)
    pallas_call x1, Pallas kernels, on_device(): pl.pallas_call(functools.partial(kernel, at), out_shape=(pltpu.VMEM(token...  43.8 us
    pallas_call x1, Pallas kernels, on_device(): pl.pallas_call(finish, out_shape=(jax.ShapeDtypeStruct(tokens.shape, BF16...  3.36 us

profile of v5, /device:TPU:0, one launch (start us, length us, event | category | flops | bytes accessed | tf_op | source)
XLA Modules:
  0.0 47.8 jit_solution(5635332191802994937)
XLA Ops:
  0.6 43.8 %shard_map.186 = (bf16[1,1024,512]{2,1,0:T(8,128)(2,1)S(1)}, bf16[1,1024,512]{2,1,0:T(8,128)(2,1)S(1)}, bf16[512,256]{1,0:T(8,128)(2,1)S(1)}, bf16[512,256]{1,0:...) custom-call(bf16[1,1024,512]{2,1,0:T(8,128)(2,1)} %tok_hbm.1, ...), custom_call_target="tpu_custom_call" | custom-call | tf_op jit(solution)/shard_map/pallas_call | solution.py:791
  44.4 3.4 %shard_map.187 = (bf16[1,1024,512]{2,1,0:T(8,128)(2,1)}, bf16[1,1024,512]{2,1,0:T(8,128)(2,1)}, f32[2,512,256]{2,1,0:T(8,128)}, f32[2,256,512]{2,1,0:T(8,128)}, ...) custom-call(bf16[1,1024,512]{2,1,0:T(8,128)(2,1)S(1)} %get-tuple-ele, ...), custom_call_target="tpu_custom_call" | custom-call | tf_op jit(solution)/shard_map/pallas_call | solution.py:852

commit v6 on v5

--- a/solution.py
+++ b/solution.py
@@ -486,8 +486,6 @@
         return carry
 
     lax.fori_loop(0, tiles, turn_u, 0)
-    for k in range(2):
-        bt[k * chan : (k + 1) * chan, :] = bw[:, k * chan : (k + 1) * chan].T
     take(cw, load_sem.at[3])
     for k in range(2):
         ct[:, k * chan : (k + 1) * chan] = cw[k * chan : (k + 1) * chan, :].T
@@ -652,6 +650,8 @@
                 if step[0] == "s":
                     small_stage(k)
                 elif step[0] == "p":
+                    for n in range(2):
+                        bt[n * chan : (n + 1) * chan, :] = bw[:, n * chan : (n + 1) * chan].T
                     lax.fori_loop(0, tiles, put_block, 0)
                 elif step[0] == "l":
                     found["gain"] = last(k, found.get("gain", jnp.zeros((8, width), F32)))

time: 48 us -> 48.7 us (1.015)
  Pallas kernels: 47.1 us -> 47.9 us
    pallas_call x1, Pallas kernels: 43.8 us -> 44.6 us  [on_device(): pl.pallas_call(functools.partial(kernel, at), out_shape=(pltpu.VMEM(token...]
where the time goes in v6:
time: 48.7 us; the launch traced here: 48.6 us
  Pallas kernels  47.9 us (98%)
  between operations  0.65 us (1%)
    pallas_call x1, Pallas kernels, on_device(): pl.pallas_call(functools.partial(kernel, at), out_shape=(pltpu.VMEM(token...  44.6 us
    pallas_call x1, Pallas kernels, on_device(): pl.pallas_call(finish, out_shape=(jax.ShapeDtypeStruct(tokens.shape, BF16...  3.36 us

profile of v6, /device:TPU:0, one launch (start us, length us, event | category | flops | bytes accessed | tf_op | source)
XLA Modules:
  0.0 48.6 jit_solution(6574944018977950939)
XLA Ops:
  0.6 44.6 %shard_map.186 = (bf16[1,1024,512]{2,1,0:T(8,128)(2,1)S(1)}, bf16[1,1024,512]{2,1,0:T(8,128)(2,1)S(1)}, bf16[512,256]{1,0:T(8,128)(2,1)S(1)}, bf16[512,256]{1,0:...) custom-call(bf16[1,1024,512]{2,1,0:T(8,128)(2,1)} %tok_hbm.1, ...), custom_call_target="tpu_custom_call" | custom-call | tf_op jit(solution)/shard_map/pallas_call | solution.py:791
  45.2 3.4 %shard_map.187 = (bf16[1,1024,512]{2,1,0:T(8,128)(2,1)}, bf16[1,1024,512]{2,1,0:T(8,128)(2,1)}, f32[2,512,256]{2,1,0:T(8,128)}, f32[2,256,512]{2,1,0:T(8,128)}, ...) custom-call(bf16[1,1024,512]{2,1,0:T(8,128)(2,1)S(1)} %get-tuple-ele, ...), custom_call_target="tpu_custom_call" | custom-call | tf_op jit(solution)/shard_map/pallas_call | solution.py:852
